TPU v7x, 32 devices: a whole 2x2x4 slice. The times are simulated.
32 devices in a mesh: fsdp: 8 (over z, y), tensor: 4 (over x, core).
Axes of the slice: x: 2, y: 2, z: 4, core: 2. Of those that a mesh axis runs over, the one named last changes fastest.
Arguments:
- layer_input: bfloat16 [2048, 8192], P('fsdp', 'tensor'), may hold values from -6 to 6
- value_grad: bfloat16 [2048, 1024], P('fsdp', 'tensor'), may hold values from -6 to 6
- quant_codes: int32 [8192, 1024], P('fsdp', 'tensor'), may hold values from 0 to 15
- block_scales: float32 [8192, 16], P('fsdp', 'tensor'), may hold values from 0.02 to 0.08
- tenant_ids: int32 [128], P('fsdp'), may hold values from 0 to 7
- live_counts: int32 [8], P('fsdp'), may hold values from 12 to 16, as said below
- tenant_owner: int32 [8], replicated, may hold values from 0 to 7, each once
- factor_down: float32 [8, 16, 8192], P('fsdp', None, 'tensor'), may hold values from -6 to 6
- factor_up: float32 [8, 16, 1024], P('fsdp', None, 'tensor'), may hold values from -6 to 6
- moment_down: float32 [8, 16, 8192], P('fsdp', None, 'tensor'), may hold values from -6 to 6
- second_down: float32 [8, 16, 8192], P('fsdp', None, 'tensor'), may hold values from 0.05 to 5
- moment_up: float32 [8, 16, 1024], P('fsdp', None, 'tensor'), may hold values from -6 to 6
- second_up: float32 [8, 16, 1024], P('fsdp', None, 'tensor'), may hold values from 0.05 to 5
Outputs:
- layer_input_gradient: bfloat16 [2048, 8192], P('fsdp', 'tensor')
- new_down: float32 [8, 16, 8192], P('fsdp', None, 'tensor')
- new_up: float32 [8, 16, 1024], P('fsdp', None, 'tensor')
- new_moment_down: float32 [8, 16, 8192], P('fsdp', None, 'tensor')
- new_second_down: float32 [8, 16, 8192], P('fsdp', None, 'tensor')
- new_moment_up: float32 [8, 16, 1024], P('fsdp', None, 'tensor')
- new_second_up: float32 [8, 16, 1024], P('fsdp', None, 'tensor')
Inputs may be any that keep to these rules, and one draw needn't show every extreme that they name: The first live_counts[f] sequence slots of fsdp index f are live and the rest are padding; some index has all 16 live. tenant_owner is a permutation: tenant t's adapter and its moments sit in slot tenant_owner[t].
All inputs are finite; a program needn't handle non-finite values.
Results may differ from a plain program's by a relative error of at most 0.01.
Values may be sent and summed in bfloat16 or wider, within the bound.
A program may use at most 128 MiB of HBM per device.

v0:
```python
import math

import jax
import jax.numpy as jnp
from jax import lax
from jax.sharding import PartitionSpec as P

MODEL_WIDTH = 8192
ADAPTER_RANK = 16


nf4_levels = (
    -1.0,
    -0.6962,
    -0.5251,
    -0.3949,
    -0.2844,
    -0.1848,
    -0.0911,
    0.0,
    0.0796,
    0.1609,
    0.2461,
    0.3379,
    0.4407,
    0.5626,
    0.723,
    1.0,
)
adapter_scale = 2.0
beta_one = 0.9
beta_two = 0.999
adam_step = 10.0
learn_rate = 0.05
decay_rate = 0.01
adam_eps = 1e-08


def adam_update(param, grad, moment, second):
    new_moment = beta_one * moment + (1.0 - beta_one) * grad
    new_second = beta_two * second + (1.0 - beta_two) * grad * grad
    corrected = new_moment / (1.0 - beta_one**adam_step)
    divisor = jnp.sqrt(new_second / (1.0 - beta_two**adam_step)) + adam_eps
    new_param = param - learn_rate * (corrected / divisor + decay_rate * param)
    return (new_param, new_moment, new_second)


def dequantize(quant_codes, block_scales):
    levels_out = jnp.zeros(quant_codes.shape, jnp.float32)
    for position in range(16):
        levels_out = jnp.where(quant_codes == position, nf4_levels[position], levels_out)
    row_count, col_count = quant_codes.shape
    blocks = block_scales.shape[1]
    scaled = levels_out.reshape(row_count, blocks, col_count // blocks) * block_scales[:, :, None]
    return scaled.reshape(row_count, col_count).astype(jnp.bfloat16)


def right_product(left, right):
    return lax.dot_general(
        left, right, (((1,), (1,)), ((), ())), preferred_element_type=jnp.float32
    )


def left_product(left, right):
    return lax.dot_general(
        left, right, (((0,), (0,)), ((), ())), preferred_element_type=jnp.float32
    )


def add_sources(pieces):
    return (jnp.sum(pieces[0], axis=0, keepdims=True), jnp.sum(pieces[1], axis=0, keepdims=True))


def shards(
    layer_input,
    value_grad,
    quant_codes,
    block_scales,
    tenant_ids,
    live_counts,
    tenant_owner,
    factor_down,
    factor_up,
    moment_down,
    second_down,
    moment_up,
    second_up,
):
    tok_rows, width_part = layer_input.shape
    value_part = value_grad.shape[1]
    slot_count = tenant_ids.shape[0]
    seq_len = tok_rows // slot_count
    tenant_total = tenant_owner.shape[0]
    rank_size = factor_down.shape[1]
    inverse_width = 1.0 / math.sqrt(MODEL_WIDTH)
    coefficient = adapter_scale / math.sqrt(ADAPTER_RANK)
    live_seq = jnp.arange(slot_count, dtype=jnp.int32) < live_counts[0]
    live_tok = jnp.broadcast_to(live_seq[:, None], (slot_count, seq_len)).reshape(tok_rows)
    masked = jnp.where(live_tok[:, None], value_grad, jnp.zeros_like(value_grad))
    tenant_iota = jnp.arange(tenant_total, dtype=jnp.int32)
    matches = tenant_ids[:, None] == tenant_iota[None, :]
    slot_seq = jnp.sum(jnp.where(matches, tenant_owner[None, :], 0), axis=1)
    onehot_seq = (slot_seq[:, None] == tenant_iota[None, :]).astype(jnp.bfloat16)
    weight_local = dequantize(quant_codes, block_scales)
    all_down, all_up = (
        lax.all_gather(factor_down.astype(jnp.bfloat16), "fsdp", axis=0, tiled=True),
        lax.all_gather(factor_up.astype(jnp.bfloat16), "fsdp", axis=0, tiled=True),
    )
    partial_value = right_product(masked, lax.all_gather(weight_local, "fsdp", axis=0, tiled=True))
    base_input_grad = lax.psum_scatter(
        partial_value.astype(jnp.bfloat16), "tensor", scatter_dimension=1, tiled=True
    ).astype(jnp.float32)
    flattened_down = all_down.reshape(tenant_total * rank_size, width_part)
    up_flat = all_up.reshape(tenant_total * rank_size, value_part)
    onehot_tok = jnp.broadcast_to(
        onehot_seq[:, None, :], (slot_count, seq_len, tenant_total)
    ).reshape(tok_rows, tenant_total)
    selector = onehot_tok.astype(jnp.float32)[:, :, None]
    down_scores = right_product(layer_input, flattened_down).reshape(
        tok_rows, tenant_total, rank_size
    )
    up_scores = right_product(masked, up_flat).reshape(tok_rows, tenant_total, rank_size)
    in_part = jnp.sum(down_scores * selector, axis=1) * inverse_width
    grad_part = jnp.sum(up_scores * selector, axis=1) * coefficient
    in_sum, grad_sum = lax.psum((in_part, grad_part), "tensor")
    input_lowrank = in_sum.astype(jnp.bfloat16)
    gradient_lowrank = grad_sum.astype(jnp.bfloat16)
    spread_gradient = (onehot_tok[:, :, None] * gradient_lowrank[:, None, :]).reshape(
        tok_rows, tenant_total * rank_size
    )
    in_spread = (onehot_tok[:, :, None] * input_lowrank[:, None, :]).reshape(
        tok_rows, tenant_total * rank_size
    )
    adapter_input_grad = (
        jnp.dot(spread_gradient, flattened_down, preferred_element_type=jnp.float32) * inverse_width
    )
    down_terms = (left_product(spread_gradient, layer_input) * inverse_width).reshape(
        tenant_total, rank_size, width_part
    )
    up_terms = (left_product(in_spread, masked) * coefficient).reshape(
        tenant_total, rank_size, value_part
    )
    down_gradient, up_gradient = add_sources(
        (
            lax.all_to_all(
                down_terms.astype(jnp.bfloat16), "fsdp", split_axis=0, concat_axis=0, tiled=True
            ).astype(down_terms.dtype),
            lax.all_to_all(
                up_terms.astype(jnp.bfloat16), "fsdp", split_axis=0, concat_axis=0, tiled=True
            ).astype(up_terms.dtype),
        )
    )
    layer_input_gradient = (base_input_grad + adapter_input_grad).astype(jnp.bfloat16)
    new_down, new_moment_down, new_second_down = adam_update(
        factor_down, down_gradient, moment_down, second_down
    )
    new_up, new_moment_up, new_second_up = adam_update(factor_up, up_gradient, moment_up, second_up)
    return (
        layer_input_gradient,
        new_down,
        new_up,
        new_moment_down,
        new_second_down,
        new_moment_up,
        new_second_up,
    )


def solution(mesh):
    in_specs = (
        P("fsdp", "tensor"),
        P("fsdp", "tensor"),
        P("fsdp", "tensor"),
        P("fsdp", "tensor"),
        P("fsdp"),
        P("fsdp"),
        P(),
        P("fsdp", None, "tensor"),
        P("fsdp", None, "tensor"),
        P("fsdp", None, "tensor"),
        P("fsdp", None, "tensor"),
        P("fsdp", None, "tensor"),
        P("fsdp", None, "tensor"),
    )
    out_specs = (
        P("fsdp", "tensor"),
        P("fsdp", None, "tensor"),
        P("fsdp", None, "tensor"),
        P("fsdp", None, "tensor"),
        P("fsdp", None, "tensor"),
        P("fsdp", None, "tensor"),
        P("fsdp", None, "tensor"),
    )
    return jax.shard_map(shards, mesh=mesh, in_specs=in_specs, out_specs=out_specs, check_vma=False)
```

profile of v0, /device:TPU:0, one launch (start us, length us, event | category | flops | bytes accessed | tf_op | source)
XLA Modules:
  0.0 206.4 jit_solution(8490748756117757900)
XLA Ops:
  7.2 1.6 copy.53
  8.9 2.7 %fusion.8 = bf16[1024,256]{0,1:T(8,128)(2,1)} fusion(s32[1024,256]{0,1:T(8,128)S(1)} %copy.53, f32[1024,4]{0,1:T(4,128)} %param.16), kind=kLoop, calls=%fused_computation.15 | loop fusion | flops 8912896 | bytes 1589248 | tf_op jit(solution)/shard_map/convert_element_type | solution.py:55
  12.3 0.1 broadcast_in_dim.98
  12.4 0.1 broadcast_in_dim.99
  12.5 75.4 %all-gather.2.cloned.1.call-done = bf16[8192,256]{0,1:T(8,128)(2,1)} async-done(((bf16[1024,256]{0,1:T(8,128)(2,1)}), bf16[8192,256]{0,1:T(8,128)(2,1)}) %all-gather.2.cloned.1.call-update) | async-done | bytes 4194320 | tf_op jit(solution)/shard_map/all_gather | solution.py:109
  87.8 5.4 %convolution_convert_fusion = bf16[256,8192]{1,0:T(8,128)(2,1)} fusion(bf16[8192,256]{0,1:T(8,128)(2,1)} %all-gather.2.cloned.1.call-done, bf16[256,256]{1,0:T(8,128)(2,1)S(1)} %copy-done.2, pred[256]{0:T(512)(128)(4,1)S(1)} %broadcast_in_dim.99), kind=kOutput, calls=%fused_computation | convolution fusion | flops 1075904512 | bytes 8519936 | tf_op jit(solution)/shard_map/dot_general | solution.py:59
  93.3 0.9 copy-done.1
  94.2 0.1 select_reduce_fusion
  94.3 0.1 broadcast_in_dim.120
  94.4 0.1 mul.218
  94.5 30.5 %all_gather.10 = bf16[8,16,256]{2,1,0:T(8,128)(2,1)S(1)} all-gather(bf16[1,16,256]{2,1,0:T(8,128)(2,1)S(1)} %convert_element_type.60), channel_id=1, replica_groups=mesh['fsdp'=8,'tensor'=4] {'fsdp'}, dimensions={0}, use_global_device_ids=true | all-gather | bytes 73728 | tf_op jit(solution)/shard_map/all_gather | solution.py:107
  125.1 0.3 fusion.6
  125.3 31.4 %all_gather.11 = bf16[8,16,2048]{2,1,0:T(8,128)(2,1)S(1)} all-gather(bf16[1,16,2048]{2,1,0:T(8,128)(2,1)S(1)} %convert_element_type.63), channel_id=1, replica_groups=mesh['fsdp'=8,'tensor'=4] {'fsdp'}, dimensions={0}, use_global_device_ids=true | all-gather | bytes 589824 | tf_op jit(solution)/shard_map/all_gather | solution.py:106
  156.8 0.5 fusion.5
  157.3 10.3 %all-reduce = (bf16[256,16]{0,1:T(8,128)(2,1)S(1)}, bf16[256,16]{0,1:T(8,128)(2,1)S(1)}) all-reduce(f32[256,16]{0,1:T(8,128)S(1)} %broadcast_multiply_fusion.3, f32[256,16]{0,1:T(8,128)S(1)} %broadcast_multiply_fusion.2), channel_id=1, replica_groups=mesh['fsdp'=8,'tensor'=4] {'tensor'}, use_global_device_ids=true, to_apply=%region_3.4 | all-reduce | flops 8192 | bytes 49152 | tf_op jit(solution)/shard_map/psum | solution.py:125
  167.6 0.9 fusion.4
  168.5 3.4 %all-to-all-start.1 = ((bf16[8,16,256]{2,1,0:T(8,128)(2,1)}), bf16[8,16,256]{2,1,0:T(8,128)(2,1)S(1)}, u32[]{:S(2)}, u32[]{:S(2)}) async-start(bf16[8,16,256]{2,1,0:T(8,128)(2,1)} %bitcast.9), calls=%async_computation.2 | async-start | bytes 131072 | tf_op jit(solution)/shard_map/all_to_all | solution.py:148
  171.8 1.1 fusion.3
  172.9 5.7 %all-to-all-done.1 = bf16[8,16,256]{2,1,0:T(8,128)(2,1)S(1)} async-done(((bf16[8,16,256]{2,1,0:T(8,128)(2,1)}), bf16[8,16,256]{2,1,0:T(8,128)(2,1)S(1)}, u32[]{:S(2)}, u32[]{:S(2)}) %all-to-all-start.1) | async-done | bytes 65568 | tf_op jit(solution)/shard_map/all_to_all | solution.py:148
  178.7 3.5 %all-to-all-start = ((bf16[8,16,2048]{2,1,0:T(8,128)(2,1)}), bf16[8,16,2048]{2,1,0:T(8,128)(2,1)S(1)}, u32[]{:S(2)}, u32[]{:S(2)}) async-start(bf16[8,16,2048]{2,1,0:T(8,128)(2,1)} %bitcast.5), calls=%async_computation.1 | async-start | bytes 1048576 | tf_op jit(solution)/shard_map/all_to_all | solution.py:145
  182.2 0.6 multiply_subtract_fusion.1
  182.9 13.2 %all-to-all-done = bf16[8,16,2048]{2,1,0:T(8,128)(2,1)S(1)} async-done(((bf16[8,16,2048]{2,1,0:T(8,128)(2,1)}), bf16[8,16,2048]{2,1,0:T(8,128)(2,1)S(1)}, u32[]{:S(2)}, u32[]{:S(2)}) %all-to-all-start) | async-done | bytes 524320 | tf_op jit(solution)/shard_map/all_to_all | solution.py:145
  196.1 0.8 multiply_subtract_fusion
  196.9 2.7 %fusion.2 = bf16[256,2048]{1,0:T(8,128)(2,1)} fusion(bf16[8,16,2048]{2,1,0:T(8,128)(2,1)S(1)} %all_gather.11, bf16[256,2048]{1,0:T(8,128)(2,1)} %reduce-scatter.2.cloned.1.call-done, bf16[256,16]{0,1:T(8,128)(2,1)S(1)} %get-tuple-element.7, bf16[256,8]{0,1:T(8,128)(2,1)S(1)} %mul.218), kind=kOutput, calls=%fused_computation.4 | convolution fusion | flops 136347648 | bytes 2633728 | tf_op jit(solution)/shard_map/dot_general | solution.py:135
  (34 shorter events, 0.3 us)
Async XLA Ops:
  7.2 149.6 %copy-start = (bf16[256,2048]{1,0:T(8,128)(2,1)S(1)}, bf16[256,2048]{1,0:T(8,128)(2,1)}, u32[]{:S(2)}) copy-start(bf16[256,2048]{1,0:T(8,128)(2,1)} %param.13) | copy-start | bytes 3145732
  7.2 80.6 %copy-start.2 = (bf16[256,256]{1,0:T(8,128)(2,1)S(1)}, bf16[256,256]{1,0:T(8,128)(2,1)}, u32[]{:S(2)}) copy-start(bf16[256,256]{1,0:T(8,128)(2,1)} %param.14) | copy-start | bytes 393220
  7.2 80.6 %all-gather.2.cloned.1.call-start = ((), (), s32[]{:S(2)}) async-start(), calls=%async_computation.3 | async-start | bytes 4718592 | tf_op jit(solution)/shard_map/all_gather | solution.py:109
  11.6 185.4 %reduce-scatter.2.cloned.1.call-start = ((), (), s32[]{:S(2)}) async-start(), calls=%async_computation.4 | async-start | bytes 5242880 | tf_op jit(solution)/shard_map/reduce_scatter | solution.py:110
  93.2 0.9 copy-start.1
  93.2 0.9 copy-start.5
  93.2 1.0 copy-start.8
  93.3 1.0 copy-start.9
  94.1 88.1 %copy-start.6 = (f32[1,16,256]{2,1,0:T(8,128)S(1)}, f32[1,16,256]{2,1,0:T(8,128)}, u32[]{:S(2)}) copy-start(f32[1,16,256]{2,1,0:T(8,128)} %param.24) | copy-start | bytes 49156
  94.2 88.1 %copy-start.7 = (f32[1,16,256]{2,1,0:T(8,128)S(1)}, f32[1,16,256]{2,1,0:T(8,128)}, u32[]{:S(2)}) copy-start(f32[1,16,256]{2,1,0:T(8,128)} %param.25) | copy-start | bytes 49156
  94.2 102.0 %copy-start.3 = (f32[1,16,2048]{2,1,0:T(8,128)S(1)}, f32[1,16,2048]{2,1,0:T(8,128)}, u32[]{:S(2)}) copy-start(f32[1,16,2048]{2,1,0:T(8,128)} %param.22) | copy-start | bytes 393220
  94.2 102.0 %copy-start.4 = (f32[1,16,2048]{2,1,0:T(8,128)S(1)}, f32[1,16,2048]{2,1,0:T(8,128)}, u32[]{:S(2)}) copy-start(f32[1,16,2048]{2,1,0:T(8,128)} %param.23) | copy-start | bytes 393220
  168.5 10.2 %all-to-all-start.1 = ((bf16[8,16,256]{2,1,0:T(8,128)(2,1)}), bf16[8,16,256]{2,1,0:T(8,128)(2,1)S(1)}, u32[]{:S(2)}, u32[]{:S(2)}) async-start(bf16[8,16,256]{2,1,0:T(8,128)(2,1)} %bitcast.9), calls=%async_computation.2 | async-start | bytes 131072 | tf_op jit(solution)/shard_map/all_to_all | solution.py:148
  178.7 17.4 %all-to-all-start = ((bf16[8,16,2048]{2,1,0:T(8,128)(2,1)}), bf16[8,16,2048]{2,1,0:T(8,128)(2,1)S(1)}, u32[]{:S(2)}, u32[]{:S(2)}) async-start(bf16[8,16,2048]{2,1,0:T(8,128)(2,1)} %bitcast.5), calls=%async_computation.1 | async-start | bytes 1048576 | tf_op jit(solution)/shard_map/all_to_all | solution.py:145
Sparse Core Ops, SparseCore 0:
  11.7 76.0 all-gather.1
  93.4 42.7 reduce-scatter.1
where the time goes:
time: 207 us; the launch traced here: 206 us
  waiting for transfers between devices  94.3 us (46%)
  blocking collectives  72.3 us (35%)
  between operations  14.9 us (7%)
  matrix products  10.8 us (5%)
  starting transfers between devices  6.93 us (3%)
  other arithmetic  4.32 us (2%)
  local copies, waits for them, and re-layouts  2.91 us (1%)
    all_gather x1, waiting for transfers between devices, shards(): lax.all_gather(weight_local, 'fsdp', axis=0, tiled=True)  75.4 us
    all_gather x1, blocking collectives, shards(): lax.all_gather(factor_down.astype(jnp.bfloat16), 'fsdp', axis=0, tiled=True)  31.4 us
    all_gather x1, blocking collectives, shards(): lax.all_gather(factor_up.astype(jnp.bfloat16), 'fsdp', axis=0, tiled=True)  30.5 us
    all_to_all x1, waiting for transfers between devices, shards(): lax.all_to_all(down_terms.astype(jnp.bfloat16), 'fsdp', split_axis=0, con...  13.2 us
    psum x1, blocking collectives, shards(): in_sum, grad_sum = lax.psum((in_part, grad_part), 'tensor')  10.3 us
    dot_general x3, matrix products, right_product(): lax.dot_general(left, right, (((1,), (1,)), ((), ())), preferred_element_...  6.19 us
    all_to_all x1, waiting for transfers between devices, shards(): lax.all_to_all(up_terms.astype(jnp.bfloat16), 'fsdp', split_axis=0, conca...  5.73 us
  transfers between devices with their start and end apart: 4, of which 3 were waited for; matrix products, arithmetic and copies ran while one was open for 2% of the time, Pallas kernels for 0%

commit v1 on v0

--- a/solution.py
+++ b/solution.py
@@ -1,8 +1,11 @@
+import functools
 import math
 
 import jax
 import jax.numpy as jnp
 from jax import lax
+from jax.experimental import pallas as pl
+from jax.experimental.pallas import tpu as pltpu
 from jax.sharding import PartitionSpec as P
 
 MODEL_WIDTH = 8192
@@ -166,7 +169,474 @@
     )
 
 
+CHUNKS = 4
+
+
+def level_tree(codes):
+    rows = [jnp.float32(level) for level in nf4_levels]
+    for bit in range(4):
+        chosen = (codes & (1 << bit)) != 0
+        rows = [jnp.where(chosen, rows[2 * n + 1], rows[2 * n]) for n in range(len(rows) // 2)]
+    return rows[0]
+
+
+def fused_kernel(
+    fsdp,
+    tensor,
+    ids_ref,
+    live_ref,
+    owner_ref,
+    x_ref,
+    dv_ref,
+    code_ref,
+    scale_ref,
+    fd_ref,
+    fu_ref,
+    md_ref,
+    sd_ref,
+    mu_ref,
+    su_ref,
+    out_ref,
+    nd_ref,
+    nu_ref,
+    nmd_ref,
+    nsd_ref,
+    nmu_ref,
+    nsu_ref,
+    fac,
+    gsend,
+    grecv,
+    dvs,
+    part,
+    col,
+    wgt,
+    outs,
+    base,
+    fac_s,
+    fac_r,
+    gr_s,
+    gr_r,
+    dv_s,
+    dvf_s,
+    dv_r,
+    part_s,
+    part_r,
+    col_s,
+    col_r,
+    wgt_s,
+    wgt_r,
+    out_s,
+    out_r,
+):
+    f = lax.axis_index("fsdp")
+    t = lax.axis_index("tensor")
+    z, y = f // 2, f % 2
+    x, c = t // 2, t % 2
+    planes, wide = fsdp // 2, tensor // 2
+    tok_rows, width = x_ref.shape
+    value = dv_ref.shape[1]
+    w_rows = code_ref.shape[0]
+    step_rows = w_rows // CHUNKS
+    rank = fd_ref.shape[1]
+    slots = ids_ref.shape[0]
+    seq = tok_rows // slots
+    flat = fsdp * rank
+    inverse_width = 1.0 / math.sqrt(MODEL_WIDTH)
+    coefficient = adapter_scale / math.sqrt(ADAPTER_RANK)
+    pending = []
+
+    def remote(src, dst, ss, rs, df, dt):
+        return pltpu.make_async_remote_copy(
+            src_ref=src,
+            dst_ref=dst,
+            send_sem=ss,
+            recv_sem=rs,
+            device_id={"fsdp": df, "tensor": dt},
+            device_id_type=pl.DeviceIdType.MESH,
+        )
+
+    def send(copy, cond=None):
+        if cond is None:
+            copy.start()
+        else:
+            pl.when(cond)(copy.start)
+        pending.append((copy, cond))
+
+    barrier = pltpu.get_barrier_semaphore()
+    chips = [(dx, dy) for dx in range(wide) for dy in range(2)]
+    greeted = 0
+    for step in range(1, fsdp):
+        pl.semaphore_signal(
+            barrier,
+            inc=1,
+            device_id={"fsdp": (f + step) % fsdp, "tensor": t},
+            device_id_type=pl.DeviceIdType.MESH,
+        )
+        greeted += 1
+    for dx, dy in chips:
+        for dc in range(2):
+            if dx == 0 and dc == 0:
+                continue
+            pl.semaphore_signal(
+                barrier,
+                inc=1,
+                device_id={
+                    "fsdp": 2 * z + (y + dy) % 2,
+                    "tensor": 2 * ((x + dx) % wide) + (c + dc) % 2,
+                },
+                device_id_type=pl.DeviceIdType.MESH,
+            )
+            greeted += 1
+
+    fac[pl.ds(f, 1), :, 0:width] = fd_ref[...].astype(jnp.bfloat16)
+    fac[pl.ds(f, 1), :, width : width + value] = fu_ref[...].astype(jnp.bfloat16)
+    tok_index = lax.broadcasted_iota(jnp.int32, (tok_rows, value), 0)
+    masked = jnp.where(
+        tok_index < live_ref[0] * seq, dv_ref[...].astype(jnp.float32), 0.0
+    ).astype(jnp.bfloat16)
+    dvs[y, t] = masked
+
+    def dequant(chunk):
+        rows = pl.ds(chunk * step_rows, step_rows)
+        levels = level_tree(code_ref[rows, :])
+        scales = scale_ref[rows, :]
+        blocks = scales.shape[1]
+        block = value // blocks
+        lane = lax.broadcasted_iota(jnp.int32, (step_rows, value), 1)
+        spread = jnp.broadcast_to(scales[:, blocks - 1 : blocks], (step_rows, value))
+        for n in reversed(range(blocks - 1)):
+            spread = jnp.where(lane < (n + 1) * block, scales[:, n : n + 1], spread)
+        col[z, rows, :] = (levels * spread).astype(jnp.bfloat16)
+
+    dequant(0)
+    pl.semaphore_wait(barrier, greeted)
+
+    def fac_copy(df, source):
+        return remote(fac.at[source], fac.at[source], fac_s.at[df], fac_r.at[source], df, t)
+
+    for step in range(1, fsdp):
+        send(fac_copy((f + step) % fsdp, f))
+
+    def dv_copy(index, dx, dy, sy, st):
+        return remote(
+            dvs.at[sy, st],
+            dvs.at[sy, st],
+            dv_s.at[index],
+            dv_r.at[sy, st],
+            2 * z + (y + dy) % 2,
+            2 * ((x + dx) % wide) + c,
+        )
+
+    def dv_forward(index, sy, st):
+        return remote(
+            dvs.at[sy, st], dvs.at[sy, st], dvf_s.at[index], dv_r.at[sy, st], f, 2 * x + 1 - c
+        )
+
+    send(dv_forward(0, y, t))
+    for index, (dx, dy) in enumerate(chips):
+        if index > 0:
+            send(dv_copy(index, dx, dy, y, t))
+
+    def col_copy(way, p, chunk):
+        rows = pl.ds(chunk * step_rows, step_rows)
+        return remote(
+            col.at[p, rows, :],
+            col.at[p, rows, :],
+            col_s.at[way, p, chunk],
+            col_r.at[p, chunk],
+            f + (2 if way == 0 else -2),
+            t,
+        )
+
+    def in_plane(p, chunk, valid):
+        rows = pl.ds(chunk * step_rows, step_rows)
+        df, dt = 2 * z + p % 2, 2 * (p // 2) + y
+        stays = jnp.logical_and(df == f, dt == t)
+
+        @pl.when(jnp.logical_and(valid, stays))
+        def _():
+            wgt[t, rows, :] = col[p, rows, :]
+
+        copy = remote(
+            col.at[p, rows, :],
+            wgt.at[t, rows, :],
+            wgt_s.at[p, chunk],
+            wgt_r.at[t, chunk],
+            df,
+            dt,
+        )
+        send(copy, jnp.logical_and(valid, jnp.logical_not(stays)))
+
+    def relay(step):
+        for s in range(planes):
+            chunk = step - s
+            if chunk < 0 or chunk >= CHUNKS:
+                continue
+            if s == 0:
+                send(col_copy(0, z, chunk), z < planes - 1)
+                send(col_copy(1, z, chunk), z > 0)
+                in_plane(z, chunk, z >= 0)
+                continue
+            for way in range(2):
+                p = z - s if way == 0 else z + s
+                valid = p >= 0 if way == 0 else p < planes
+                further = z < planes - 1 if way == 0 else z > 0
+                held = jnp.clip(p, 0, planes - 1)
+                pl.when(valid)(col_copy(way, held, chunk).wait_recv)
+                send(col_copy(way, held, chunk), jnp.logical_and(valid, further))
+                in_plane(held, chunk, valid)
+
+    relay(0)
+    dequant(1)
+    relay(1)
+
+    for index, (dx, dy) in enumerate(chips):
+        if index > 0:
+            sy, st = (y + dy) % 2, 2 * ((x + dx) % wide) + c
+            dv_copy(index, dx, dy, sy, st).wait_recv()
+            send(dv_forward(index, sy, st))
+
+    slot_row = jnp.zeros((1, tok_rows), jnp.int32)
+    seq_row = lax.broadcasted_iota(jnp.int32, (1, tok_rows), 1) // seq
+    for n in range(slots):
+        own = jnp.int32(0)
+        for u in range(fsdp):
+            own = own + jnp.where(ids_ref[n] == u, owner_ref[u], 0)
+        slot_row = jnp.where(seq_row == n, own, slot_row)
+    named = lax.broadcasted_iota(jnp.int32, (flat, tok_rows), 0) // rank
+    chosen = named == jnp.broadcast_to(slot_row, (flat, tok_rows))
+
+    for step in range(1, fsdp):
+        source = (f + step) % fsdp
+        fac_copy(source, source).wait_recv()
+    all_down = fac[:, :, 0:width].reshape(flat, width)
+    all_up = fac[:, :, width : width + value].reshape(flat, value)
+
+    def folded(scores, factor):
+        kept = jnp.where(chosen, scores, 0.0).reshape(fsdp, rank, tok_rows)
+        return jnp.sum(kept, axis=0) * factor
+
+    part[t, 0:rank, :] = folded(right_product(all_down, x_ref[...]), inverse_width)
+    part[t, rank : 2 * rank, :] = folded(right_product(all_up, masked), coefficient)
+
+    def part_copy(dt, source):
+        return remote(part.at[source], part.at[source], part_s.at[dt], part_r.at[source], f, dt)
+
+    for step in range(1, tensor):
+        send(part_copy((t + step) % tensor, t))
+
+    dequant(2)
+    relay(2)
+    dequant(3)
+
+    for step in range(1, tensor):
+        source = (t + step) % tensor
+        part_copy(source, source).wait_recv()
+    sums = jnp.sum(part[...], axis=0)
+    low = sums.astype(jnp.bfloat16).astype(jnp.float32)
+
+    def spread_out(rows):
+        tiled = jnp.broadcast_to(rows[None], (fsdp, rank, tok_rows)).reshape(flat, tok_rows)
+        return jnp.where(chosen, tiled, 0.0).astype(jnp.bfloat16)
+
+    in_spread = spread_out(low[0:rank])
+    grad_spread = spread_out(low[rank : 2 * rank])
+    down_terms = jnp.dot(grad_spread, x_ref[...], preferred_element_type=jnp.float32)
+    gsend[:, :, 0:width] = (
+        (down_terms * inverse_width).astype(jnp.bfloat16).reshape(fsdp, rank, width)
+    )
+    up_terms = jnp.dot(in_spread, masked, preferred_element_type=jnp.float32)
+    gsend[:, :, width : width + value] = (
+        (up_terms * coefficient).astype(jnp.bfloat16).reshape(fsdp, rank, value)
+    )
+
+    def grad_copy(df, source):
+        return remote(gsend.at[df], grecv.at[source], gr_s.at[df], gr_r.at[source], df, t)
+
+    for step in range(1, fsdp):
+        send(grad_copy((f + step) % fsdp, f))
+    grecv[pl.ds(f, 1)] = gsend[pl.ds(f, 1)]
+
+    relay(3)
+
+    for sy in range(2):
+        for st in range(tensor):
+            pl.when(st % 2 != c)(dv_forward(0, sy, st).wait_recv)
+
+    def multiply(chunk):
+        rows = pl.ds(chunk * step_rows, step_rows)
+        for st in range(tensor):
+            stays = jnp.logical_and(c == y, t == st)
+            arrived = remote(
+                col.at[0, rows, :],
+                wgt.at[st, rows, :],
+                wgt_s.at[0, chunk],
+                wgt_r.at[st, chunk],
+                f,
+                t,
+            )
+            pl.when(jnp.logical_not(stays))(arrived.wait_recv)
+        for half in range(2):
+            total = right_product(dvs[half, 0], wgt[0, rows, :])
+            for st in range(1, tensor):
+                total = total + right_product(dvs[half, st], wgt[st, rows, :])
+            outs[half, chunk] = total.astype(jnp.bfloat16)
+            df, dt = 2 * z + half, 2 * x + y
+            stays = jnp.logical_and(df == f, dt == t)
+
+            @pl.when(stays)
+            def _():
+                base[c, chunk] = outs[half, chunk]
+
+            copy = remote(
+                outs.at[half, chunk],
+                base.at[c, chunk],
+                out_s.at[half, chunk],
+                out_r.at[c, chunk],
+                df,
+                dt,
+            )
+            send(copy, jnp.logical_not(stays))
+
+    for step in range(planes, CHUNKS + planes - 1):
+        relay(step)
+        multiply(step - planes)
+
+    for step in range(1, fsdp):
+        source = (f + step) % fsdp
+        grad_copy(source, source).wait_recv()
+    multiply(CHUNKS - 1)
+
+    down_grad = jnp.sum(grecv[:, :, 0:width].astype(jnp.float32), axis=0, keepdims=True)
+    up_grad = jnp.sum(
+        grecv[:, :, width : width + value].astype(jnp.float32), axis=0, keepdims=True
+    )
+    nd_ref[...], nmd_ref[...], nsd_ref[...] = adam_update(
+        fd_ref[...], down_grad, md_ref[...], sd_ref[...]
+    )
+    nu_ref[...], nmu_ref[...], nsu_ref[...] = adam_update(
+        fu_ref[...], up_grad, mu_ref[...], su_ref[...]
+    )
+
+    for chunk in range(CHUNKS):
+        for half in range(2):
+            stays = jnp.logical_and(half == c, c == f % 2)
+            arrived = remote(
+                outs.at[0, chunk],
+                base.at[half, chunk],
+                out_s.at[0, chunk],
+                out_r.at[half, chunk],
+                f,
+                t,
+            )
+            pl.when(jnp.logical_not(stays))(arrived.wait_recv)
+            start = half * w_rows + chunk * step_rows
+            low_term = lax.dot_general(
+                grad_spread,
+                fac[:, :, start : start + step_rows].reshape(flat, step_rows),
+                (((0,), (0,)), ((), ())),
+                preferred_element_type=jnp.float32,
+            )
+            out_ref[:, start : start + step_rows] = (
+                base[half, chunk].astype(jnp.float32) + low_term * inverse_width
+            ).astype(jnp.bfloat16)
+
+    for copy, cond in pending:
+        if cond is None:
+            copy.wait_send()
+        else:
+            pl.when(cond)(copy.wait_send)
+
+
+def fused(fsdp, tensor, *args):
+    (
+        layer_input,
+        value_grad,
+        quant_codes,
+        block_scales,
+        tenant_ids,
+        live_counts,
+        tenant_owner,
+        factor_down,
+        factor_up,
+        moment_down,
+        second_down,
+        moment_up,
+        second_up,
+    ) = args
+    tok_rows, width = layer_input.shape
+    value = value_grad.shape[1]
+    w_rows = quant_codes.shape[0]
+    rank = factor_down.shape[1]
+    step_rows = w_rows // CHUNKS
+    low = jnp.bfloat16
+    dma = pltpu.SemaphoreType.DMA
+    smem = pl.BlockSpec(memory_space=pltpu.SMEM)
+    vmem = pl.BlockSpec(memory_space=pltpu.VMEM)
+    like = jax.ShapeDtypeStruct
+    return pl.pallas_call(
+        functools.partial(fused_kernel, fsdp, tensor),
+        out_shape=(
+            like(layer_input.shape, low),
+            like(factor_down.shape, jnp.float32),
+            like(factor_up.shape, jnp.float32),
+            like(factor_down.shape, jnp.float32),
+            like(factor_down.shape, jnp.float32),
+            like(factor_up.shape, jnp.float32),
+            like(factor_up.shape, jnp.float32),
+        ),
+        in_specs=[smem] * 3 + [vmem] * 10,
+        out_specs=(vmem,) * 7,
+        scratch_shapes=[
+            pltpu.VMEM((fsdp, rank, width + value), low),
+            pltpu.VMEM((fsdp, rank, width + value), low),
+            pltpu.VMEM((fsdp, rank, width + value), low),
+            pltpu.VMEM((2, tensor, tok_rows, value), low),
+            pltpu.VMEM((tensor, 2 * rank, tok_rows), jnp.float32),
+            pltpu.VMEM((fsdp // 2, w_rows, value), low),
+            pltpu.VMEM((tensor, w_rows, value), low),
+            pltpu.VMEM((2, CHUNKS, tok_rows, step_rows), low),
+            pltpu.VMEM((2, CHUNKS, tok_rows, step_rows), low),
+            dma((fsdp,)),
+            dma((fsdp,)),
+            dma((fsdp,)),
+            dma((fsdp,)),
+            dma((tensor,)),
+            dma((tensor,)),
+            dma((2, tensor)),
+            dma((tensor,)),
+            dma((tensor,)),
+            dma((2, fsdp // 2, CHUNKS)),
+            dma((fsdp // 2, CHUNKS)),
+            dma((fsdp // 2, CHUNKS)),
+            dma((tensor, CHUNKS)),
+            dma((2, CHUNKS)),
+            dma((2, CHUNKS)),
+        ],
+        compiler_params=pltpu.CompilerParams(
+            collective_id=0, has_side_effects=True, vmem_limit_bytes=40 * 1024 * 1024
+        ),
+    )(
+        tenant_ids,
+        live_counts,
+        tenant_owner,
+        layer_input,
+        value_grad,
+        quant_codes,
+        block_scales,
+        factor_down,
+        factor_up,
+        moment_down,
+        second_down,
+        moment_up,
+        second_up,
+    )
+
+
 def solution(mesh):
+    fsdp, tensor = mesh.shape["fsdp"], mesh.shape["tensor"]
+    planar = fsdp == 2 * tensor and tensor % 2 == 0
+    body = functools.partial(fused, fsdp, tensor) if planar else shards
     in_specs = (
         P("fsdp", "tensor"),
         P("fsdp", "tensor"),
@@ -191,4 +661,4 @@
         P("fsdp", None, "tensor"),
         P("fsdp", None, "tensor"),
     )
-    return jax.shard_map(shards, mesh=mesh, in_specs=in_specs, out_specs=out_specs, check_vma=False)
+    return jax.shard_map(body, mesh=mesh, in_specs=in_specs, out_specs=out_specs, check_vma=False)

time: 207 us -> 95.8 us (0.46)
  the two profiles are of different devices: /device:TPU:0 before, /device:TPU:3 now
where the time goes in v1:
time: 95.8 us; the launch traced here: 95.4 us
  Pallas kernels  83 us (87%)
  local copies, waits for them, and re-layouts  11 us (11%)
  between operations  1.37 us (1%)
    pallas_call x1, Pallas kernels, fused(): pl.pallas_call(functools.partial(fused_kernel, fsdp, tensor), out_shape=(...  83 us
    unnamed x30, local copies, waits for them, and re-layouts  11 us

profile of v1, /device:TPU:3, one launch (start us, length us, event | category | flops | bytes accessed | tf_op | source)
XLA Modules:
  0.0 95.4 jit_solution(3045564684362204726)
XLA Ops:
  1.3 0.0 copy-start.2
  1.3 0.0 copy-start.3
  1.3 0.0 copy-start.4
  1.3 0.0 copy-start.5
  1.3 0.0 copy-start.6
  1.3 1.0 %copy.20.scale_ref = f32[1024,4]{1,0:T(8,128)S(1)} copy(f32[1024,4]{0,1:T(4,128)} %param.16) | data formatting | bytes 32768 | tf_op args[3]
  2.3 0.0 copy-done.2
  2.3 0.0 copy-done.3
  2.4 0.0 copy-done.4
  2.4 0.0 copy-done.5
  2.4 1.2 %copy-done = bf16[256,2048]{1,0:T(8,128)(2,1)S(1)} copy-done((bf16[256,2048]{1,0:T(8,128)(2,1)S(1)}, bf16[256,2048]{1,0:T(8,128)(2,1)}, u32[]{:S(2)}) %copy-start) | copy-done | bytes 1048600
  3.6 1.2 %copy-done.1 = s32[1024,256]{1,0:T(8,128)S(1)} copy-done((s32[1024,256]{1,0:T(8,128)S(1)}, s32[1024,256]{1,0:T(8,128)}, u32[]{:S(2)}) %copy-start.1) | copy-done | bytes 1048600
  4.9 0.7 copy-done.7
  5.6 0.7 copy-done.8
  6.3 0.7 copy-done.9
  6.9 0.7 copy-done.10
  7.6 83.0 %shard_map.180 = (bf16[256,2048]{1,0:T(8,128)(2,1)S(1)}, f32[1,16,2048]{2,1,0:T(8,128)S(1)}, f32[1,16,256]{2,1,0:T(8,128)S(1)}, f32[1,16,2048]{2,1,0:T(8,128)S(1...) custom-call(s32[16]{0:T(128)S(1)} %copy-done.9, s32[1]{0:T(128)S(6)} %copy.28.live_ref, ...), custom_call_target="tpu_custom_call" | custom-call | tf_op jit(solution)/shard_map/pallas_call | solution.py:577
  90.6 1.0 %copy.29 = bf16[256,2048]{1,0:T(8,128)(2,1)} copy(bf16[256,2048]{1,0:T(8,128)(2,1)S(1)} %get-tuple-element.14) | data formatting | bytes 2097152
  91.6 0.7 copy.30
  92.2 0.6 copy.31
  92.8 0.7 copy.32
  93.5 0.7 copy.33
  94.1 0.6 copy.34
  94.7 0.6 copy.35
  (7 shorter events, 0.0 us)
Async XLA Ops:
  1.3 1.1 %copy-start.2 = (bf16[256,256]{1,0:T(8,128)(2,1)S(1)}, bf16[256,256]{1,0:T(8,128)(2,1)}, u32[]{:S(2)}) copy-start(bf16[256,256]{1,0:T(8,128)(2,1)} %dv_ref.1) | copy-start | bytes 393220
  1.3 1.1 %copy-start.3 = (f32[1,16,2048]{2,1,0:T(8,128)S(1)}, f32[1,16,2048]{2,1,0:T(8,128)}, u32[]{:S(2)}) copy-start(f32[1,16,2048]{2,1,0:T(8,128)} %fd_ref.1) | copy-start | bytes 393220
  1.3 1.1 %copy-start.4 = (f32[1,16,2048]{2,1,0:T(8,128)S(1)}, f32[1,16,2048]{2,1,0:T(8,128)}, u32[]{:S(2)}) copy-start(f32[1,16,2048]{2,1,0:T(8,128)} %md_ref.1) | copy-start | bytes 393220
  1.3 1.1 %copy-start.5 = (f32[1,16,2048]{2,1,0:T(8,128)S(1)}, f32[1,16,2048]{2,1,0:T(8,128)}, u32[]{:S(2)}) copy-start(f32[1,16,2048]{2,1,0:T(8,128)} %sd_ref.1) | copy-start | bytes 393220
  1.3 1.1 %copy-start.6 = (f32[1,16,256]{2,1,0:T(8,128)S(1)}, f32[1,16,256]{2,1,0:T(8,128)}, u32[]{:S(2)}) copy-start(f32[1,16,256]{2,1,0:T(8,128)} %fu_ref.1) | copy-start | bytes 49156
  2.4 1.2 %copy-start = (bf16[256,2048]{1,0:T(8,128)(2,1)S(1)}, bf16[256,2048]{1,0:T(8,128)(2,1)}, u32[]{:S(2)}) copy-start(bf16[256,2048]{1,0:T(8,128)(2,1)} %x_ref.1) | copy-start | bytes 3145732
  3.6 1.2 %copy-start.1 = (s32[1024,256]{1,0:T(8,128)S(1)}, s32[1024,256]{1,0:T(8,128)}, u32[]{:S(2)}) copy-start(s32[1024,256]{1,0:T(8,128)} %code_ref.1) | copy-start | bytes 3145732
  4.9 0.7 copy-start.7
  5.6 0.7 copy-start.8
  6.3 0.7 copy-start.9
  6.9 0.7 copy-start.10

commit v2 on v1

--- a/solution.py
+++ b/solution.py
@@ -183,6 +183,18 @@
 def fused_kernel(
     fsdp,
     tensor,
+    ids_any,
+    live_any,
+    owner_any,
+    x_any,
+    dv_any,
+    code_any,
+    scale_any,
+    fd_any,
+    fu_any,
+    out_ref,
+    dg_ref,
+    ug_ref,
     ids_ref,
     live_ref,
     owner_ref,
@@ -192,19 +204,11 @@
     scale_ref,
     fd_ref,
     fu_ref,
-    md_ref,
-    sd_ref,
-    mu_ref,
-    su_ref,
-    out_ref,
-    nd_ref,
-    nu_ref,
-    nmd_ref,
-    nsd_ref,
-    nmu_ref,
-    nsu_ref,
+    in_s,
     fac,
     gsend,
+    gy,
+    gz,
     grecv,
     dvs,
     part,
@@ -213,9 +217,12 @@
     outs,
     base,
     fac_s,
+    fac_f,
     fac_r,
-    gr_s,
-    gr_r,
+    gy_s,
+    gy_r,
+    gz_s,
+    gz_r,
     dv_s,
     dvf_s,
     dv_r,
@@ -245,6 +252,23 @@
     coefficient = adapter_scale / math.sqrt(ADAPTER_RANK)
     pending = []
 
+    loads = {}
+    for n, (name, src, dst) in enumerate(
+        (
+            ("fd", fd_any, fd_ref),
+            ("fu", fu_any, fu_ref),
+            ("dv", dv_any, dv_ref),
+            ("live", live_any, live_ref),
+            ("scale", scale_any, scale_ref),
+            ("code", code_any, code_ref),
+            ("x", x_any, x_ref),
+            ("ids", ids_any, ids_ref),
+            ("owner", owner_any, owner_ref),
+        )
+    ):
+        loads[name] = pltpu.make_async_copy(src, dst, in_s.at[n])
+        loads[name].start()
+
     def remote(src, dst, ss, rs, df, dt):
         return pltpu.make_async_remote_copy(
             src_ref=src,
@@ -288,18 +312,22 @@
             )
             greeted += 1
 
+    loads["fd"].wait()
+    loads["fu"].wait()
     fac[pl.ds(f, 1), :, 0:width] = fd_ref[...].astype(jnp.bfloat16)
     fac[pl.ds(f, 1), :, width : width + value] = fu_ref[...].astype(jnp.bfloat16)
+    loads["dv"].wait()
+    loads["live"].wait()
     tok_index = lax.broadcasted_iota(jnp.int32, (tok_rows, value), 0)
     masked = jnp.where(
         tok_index < live_ref[0] * seq, dv_ref[...].astype(jnp.float32), 0.0
     ).astype(jnp.bfloat16)
-    dvs[y, t] = masked
+    dvs[t, y] = masked
 
     def dequant(chunk):
         rows = pl.ds(chunk * step_rows, step_rows)
         levels = level_tree(code_ref[rows, :])
-        scales = scale_ref[rows, :]
+        scales = jnp.transpose(scale_ref[:, rows])
         blocks = scales.shape[1]
         block = value // blocks
         lane = lax.broadcasted_iota(jnp.int32, (step_rows, value), 1)
@@ -308,34 +336,42 @@
             spread = jnp.where(lane < (n + 1) * block, scales[:, n : n + 1], spread)
         col[z, rows, :] = (levels * spread).astype(jnp.bfloat16)
 
-    dequant(0)
     pl.semaphore_wait(barrier, greeted)
 
-    def fac_copy(df, source):
-        return remote(fac.at[source], fac.at[source], fac_s.at[df], fac_r.at[source], df, t)
-
-    for step in range(1, fsdp):
-        send(fac_copy((f + step) % fsdp, f))
-
-    def dv_copy(index, dx, dy, sy, st):
+    def fac_copy(dz, source):
         return remote(
-            dvs.at[sy, st],
-            dvs.at[sy, st],
-            dv_s.at[index],
-            dv_r.at[sy, st],
-            2 * z + (y + dy) % 2,
+            fac.at[source], fac.at[source], fac_s.at[dz], fac_r.at[source], (f + 2 * dz) % fsdp, t
+        )
+
+    def fac_forward(dz, source):
+        return remote(
+            fac.at[source], fac.at[source], fac_f.at[dz], fac_r.at[source], 2 * z + 1 - y, t
+        )
+
+    for dz in range(1, planes):
+        send(fac_copy(dz, f))
+    send(fac_forward(0, f))
+
+    across = remote(
+        dvs.at[t, y], dvs.at[t, y], dv_s.at[0], dv_r.at[t, y], 2 * z + 1 - y, t
+    )
+    across_in = remote(
+        dvs.at[t, 1 - y], dvs.at[t, 1 - y], dv_s.at[0], dv_r.at[t, 1 - y], 2 * z + 1 - y, t
+    )
+    send(across)
+
+    def dv_copy(dx, st):
+        return remote(
+            dvs.at[st],
+            dvs.at[st],
+            dv_s.at[dx],
+            dv_r.at[st, 0],
+            f,
             2 * ((x + dx) % wide) + c,
         )
 
-    def dv_forward(index, sy, st):
-        return remote(
-            dvs.at[sy, st], dvs.at[sy, st], dvf_s.at[index], dv_r.at[sy, st], f, 2 * x + 1 - c
-        )
-
-    send(dv_forward(0, y, t))
-    for index, (dx, dy) in enumerate(chips):
-        if index > 0:
-            send(dv_copy(index, dx, dy, y, t))
+    def dv_forward(dx, st):
+        return remote(dvs.at[st], dvs.at[st], dvf_s.at[dx], dv_r.at[st, 0], f, 2 * x + 1 - c)
 
     def col_copy(way, p, chunk):
         rows = pl.ds(chunk * step_rows, step_rows)
@@ -367,15 +403,15 @@
         )
         send(copy, jnp.logical_and(valid, jnp.logical_not(stays)))
 
+    def own(chunk):
+        send(col_copy(0, z, chunk), z < planes - 1)
+        send(col_copy(1, z, chunk), z > 0)
+        in_plane(z, chunk, z >= 0)
+
     def relay(step):
-        for s in range(planes):
+        for s in range(1, planes):
             chunk = step - s
             if chunk < 0 or chunk >= CHUNKS:
-                continue
-            if s == 0:
-                send(col_copy(0, z, chunk), z < planes - 1)
-                send(col_copy(1, z, chunk), z > 0)
-                in_plane(z, chunk, z >= 0)
                 continue
             for way in range(2):
                 p = z - s if way == 0 else z + s
@@ -386,16 +422,24 @@
                 send(col_copy(way, held, chunk), jnp.logical_and(valid, further))
                 in_plane(held, chunk, valid)
 
-    relay(0)
-    dequant(1)
+    loads["scale"].wait()
+    loads["code"].wait()
+    for chunk in range(CHUNKS):
+        dequant(chunk)
+        own(chunk)
+
+    for dz in range(1, planes):
+        source = (f + 2 * dz) % fsdp
+        fac_copy(dz, source).wait_recv()
+        send(fac_forward(dz, source))
+    across_in.wait_recv()
+    for dx in range(1, wide):
+        send(dv_copy(dx, t))
+    send(dv_forward(0, t))
     relay(1)
 
-    for index, (dx, dy) in enumerate(chips):
-        if index > 0:
-            sy, st = (y + dy) % 2, 2 * ((x + dx) % wide) + c
-            dv_copy(index, dx, dy, sy, st).wait_recv()
-            send(dv_forward(index, sy, st))
-
+    loads["ids"].wait()
+    loads["owner"].wait()
     slot_row = jnp.zeros((1, tok_rows), jnp.int32)
     seq_row = lax.broadcasted_iota(jnp.int32, (1, tok_rows), 1) // seq
     for n in range(slots):
@@ -406,9 +450,11 @@
     named = lax.broadcasted_iota(jnp.int32, (flat, tok_rows), 0) // rank
     chosen = named == jnp.broadcast_to(slot_row, (flat, tok_rows))
 
-    for step in range(1, fsdp):
-        source = (f + step) % fsdp
-        fac_copy(source, source).wait_recv()
+    relay(2)
+    for dz in range(planes):
+        source = (2 * z + 2 * dz) % fsdp + 1 - y
+        fac_forward(dz, source).wait_recv()
+    loads["x"].wait()
     all_down = fac[:, :, 0:width].reshape(flat, width)
     all_up = fac[:, :, width : width + value].reshape(flat, value)
 
@@ -425,9 +471,11 @@
     for step in range(1, tensor):
         send(part_copy((t + step) % tensor, t))
 
-    dequant(2)
-    relay(2)
-    dequant(3)
+    relay(3)
+    for dx in range(1, wide):
+        st = 2 * ((x + dx) % wide) + c
+        dv_copy(dx, st).wait_recv()
+        send(dv_forward(dx, st))
 
     for step in range(1, tensor):
         source = (t + step) % tensor
@@ -442,26 +490,23 @@
     in_spread = spread_out(low[0:rank])
     grad_spread = spread_out(low[rank : 2 * rank])
     down_terms = jnp.dot(grad_spread, x_ref[...], preferred_element_type=jnp.float32)
-    gsend[:, :, 0:width] = (
-        (down_terms * inverse_width).astype(jnp.bfloat16).reshape(fsdp, rank, width)
-    )
+    by_slot = (down_terms * inverse_width).astype(jnp.bfloat16).reshape(fsdp, rank, width)
     up_terms = jnp.dot(in_spread, masked, preferred_element_type=jnp.float32)
-    gsend[:, :, width : width + value] = (
-        (up_terms * coefficient).astype(jnp.bfloat16).reshape(fsdp, rank, value)
-    )
-
-    def grad_copy(df, source):
-        return remote(gsend.at[df], grecv.at[source], gr_s.at[df], gr_r.at[source], df, t)
-
-    for step in range(1, fsdp):
-        send(grad_copy((f + step) % fsdp, f))
-    grecv[pl.ds(f, 1)] = gsend[pl.ds(f, 1)]
-
-    relay(3)
-
-    for sy in range(2):
-        for st in range(tensor):
-            pl.when(st % 2 != c)(dv_forward(0, sy, st).wait_recv)
+    up_slot = (up_terms * coefficient).astype(jnp.bfloat16).reshape(fsdp, rank, value)
+    for slot in range(fsdp):
+        gsend[slot % 2, slot // 2, :, 0:width] = by_slot[slot]
+        gsend[slot % 2, slot // 2, :, width : width + value] = up_slot[slot]
+    over = remote(gsend.at[1 - y], gy, gy_s.at[0], gy_r.at[0], 2 * z + 1 - y, t)
+    send(over)
+
+    def grad_copy(dz, to, source):
+        return remote(
+            gz.at[to], grecv.at[source], gz_s.at[dz], gz_r.at[source], (f + 2 * dz) % fsdp, t
+        )
+
+    relay(4)
+    for st in range(tensor):
+        pl.when(st % 2 != c)(dv_forward(0, st).wait_recv)
 
     def multiply(chunk):
         rows = pl.ds(chunk * step_rows, step_rows)
@@ -477,9 +522,9 @@
             )
             pl.when(jnp.logical_not(stays))(arrived.wait_recv)
         for half in range(2):
-            total = right_product(dvs[half, 0], wgt[0, rows, :])
+            total = right_product(dvs[0, half], wgt[0, rows, :])
             for st in range(1, tensor):
-                total = total + right_product(dvs[half, st], wgt[st, rows, :])
+                total = total + right_product(dvs[st, half], wgt[st, rows, :])
             outs[half, chunk] = total.astype(jnp.bfloat16)
             df, dt = 2 * z + half, 2 * x + y
             stays = jnp.logical_and(df == f, dt == t)
@@ -498,25 +543,24 @@
             )
             send(copy, jnp.logical_not(stays))
 
-    for step in range(planes, CHUNKS + planes - 1):
+    multiply(0)
+    over.wait_recv()
+    gz[...] = (gsend[y].astype(jnp.float32) + gy[...].astype(jnp.float32)).astype(jnp.bfloat16)
+    for dz in range(1, planes):
+        send(grad_copy(dz, (z + dz) % planes, z))
+    grecv[pl.ds(z, 1)] = gz[pl.ds(z, 1)]
+
+    for step in range(5, CHUNKS + planes):
         relay(step)
-        multiply(step - planes)
-
-    for step in range(1, fsdp):
-        source = (f + step) % fsdp
-        grad_copy(source, source).wait_recv()
+        if step - planes < CHUNKS - 1:
+            multiply(step - planes)
+    for dz in range(1, planes):
+        grad_copy(dz, 0, (z + dz) % planes).wait_recv()
+    dg_ref[...] = jnp.sum(grecv[:, :, 0:width].astype(jnp.float32), axis=0, keepdims=True)
+    ug_ref[...] = jnp.sum(
+        grecv[:, :, width : width + value].astype(jnp.float32), axis=0, keepdims=True
+    )
     multiply(CHUNKS - 1)
-
-    down_grad = jnp.sum(grecv[:, :, 0:width].astype(jnp.float32), axis=0, keepdims=True)
-    up_grad = jnp.sum(
-        grecv[:, :, width : width + value].astype(jnp.float32), axis=0, keepdims=True
-    )
-    nd_ref[...], nmd_ref[...], nsd_ref[...] = adam_update(
-        fd_ref[...], down_grad, md_ref[...], sd_ref[...]
-    )
-    nu_ref[...], nmu_ref[...], nsu_ref[...] = adam_update(
-        fu_ref[...], up_grad, mu_ref[...], su_ref[...]
-    )
 
     for chunk in range(CHUNKS):
         for half in range(2):
@@ -571,39 +615,49 @@
     step_rows = w_rows // CHUNKS
     low = jnp.bfloat16
     dma = pltpu.SemaphoreType.DMA
-    smem = pl.BlockSpec(memory_space=pltpu.SMEM)
     vmem = pl.BlockSpec(memory_space=pltpu.VMEM)
     like = jax.ShapeDtypeStruct
-    return pl.pallas_call(
+    layer_input_gradient, down_gradient, up_gradient = pl.pallas_call(
         functools.partial(fused_kernel, fsdp, tensor),
         out_shape=(
             like(layer_input.shape, low),
             like(factor_down.shape, jnp.float32),
             like(factor_up.shape, jnp.float32),
-            like(factor_down.shape, jnp.float32),
-            like(factor_down.shape, jnp.float32),
-            like(factor_up.shape, jnp.float32),
-            like(factor_up.shape, jnp.float32),
         ),
-        in_specs=[smem] * 3 + [vmem] * 10,
-        out_specs=(vmem,) * 7,
+        in_specs=[pl.BlockSpec(memory_space=pl.ANY)] * 9,
+        out_specs=(vmem,) * 3,
         scratch_shapes=[
+            pltpu.SMEM(tenant_ids.shape, jnp.int32),
+            pltpu.SMEM(live_counts.shape, jnp.int32),
+            pltpu.SMEM(tenant_owner.shape, jnp.int32),
+            pltpu.VMEM(layer_input.shape, low),
+            pltpu.VMEM(value_grad.shape, low),
+            pltpu.VMEM(quant_codes.shape, jnp.int32),
+            pltpu.VMEM(block_scales.shape[::-1], jnp.float32),
+            pltpu.VMEM(factor_down.shape, jnp.float32),
+            pltpu.VMEM(factor_up.shape, jnp.float32),
+            dma((9,)),
             pltpu.VMEM((fsdp, rank, width + value), low),
-            pltpu.VMEM((fsdp, rank, width + value), low),
-            pltpu.VMEM((fsdp, rank, width + value), low),
-            pltpu.VMEM((2, tensor, tok_rows, value), low),
+            pltpu.VMEM((2, fsdp // 2, rank, width + value), low),
+            pltpu.VMEM((fsdp // 2, rank, width + value), low),
+            pltpu.VMEM((fsdp // 2, rank, width + value), low),
+            pltpu.VMEM((fsdp // 2, rank, width + value), low),
+            pltpu.VMEM((tensor, 2, tok_rows, value), low),
             pltpu.VMEM((tensor, 2 * rank, tok_rows), jnp.float32),
             pltpu.VMEM((fsdp // 2, w_rows, value), low),
             pltpu.VMEM((tensor, w_rows, value), low),
             pltpu.VMEM((2, CHUNKS, tok_rows, step_rows), low),
             pltpu.VMEM((2, CHUNKS, tok_rows, step_rows), low),
+            dma((fsdp // 2,)),
+            dma((fsdp // 2,)),
             dma((fsdp,)),
-            dma((fsdp,)),
-            dma((fsdp,)),
-            dma((fsdp,)),
-            dma((tensor,)),
-            dma((tensor,)),
-            dma((2, tensor)),
+            dma((1,)),
+            dma((1,)),
+            dma((fsdp // 2,)),
+            dma((fsdp // 2,)),
+            dma((tensor // 2,)),
+            dma((tensor // 2,)),
+            dma((tensor, 2)),
             dma((tensor,)),
             dma((tensor,)),
             dma((2, fsdp // 2, CHUNKS)),
@@ -614,7 +668,7 @@
             dma((2, CHUNKS)),
         ],
         compiler_params=pltpu.CompilerParams(
-            collective_id=0, has_side_effects=True, vmem_limit_bytes=40 * 1024 * 1024
+            collective_id=0, has_side_effects=True, vmem_limit_bytes=56 * 1024 * 1024
         ),
     )(
         tenant_ids,
@@ -623,13 +677,22 @@
         layer_input,
         value_grad,
         quant_codes,
-        block_scales,
+        block_scales.T,
         factor_down,
         factor_up,
-        moment_down,
-        second_down,
-        moment_up,
-        second_up,
+    )
+    new_down, new_moment_down, new_second_down = adam_update(
+        factor_down, down_gradient, moment_down, second_down
+    )
+    new_up, new_moment_up, new_second_up = adam_update(factor_up, up_gradient, moment_up, second_up)
+    return (
+        layer_input_gradient,
+        new_down,
+        new_up,
+        new_moment_down,
+        new_second_down,
+        new_moment_up,
+        new_second_up,
     )
 
 

time: 95.8 us -> 88.7 us (0.926)
  the two profiles are of different devices: /device:TPU:3 before, /device:TPU:6 now
where the time goes in v2:
time: 88.7 us; the launch traced here: 88.5 us
  Pallas kernels  82.9 us (93%)
  other arithmetic  3.14 us (4%)
  between operations  1.38 us (2%)
  local copies, waits for them, and re-layouts  1 us (1%)
    pallas_call x1, Pallas kernels, fused(): pl.pallas_call(functools.partial(fused_kernel, fsdp, tensor), out_shape=(...  82.9 us
    sub x2, other arithmetic, adam_update(): new_param = param - learn_rate * (corrected / divisor + decay_rate * param)  3.14 us

profile of v2, /device:TPU:6, one launch (start us, length us, event | category | flops | bytes accessed | tf_op | source)
XLA Modules:
  0.0 88.5 jit_solution(5127038168839842519)
XLA Ops:
  1.3 0.0 copy-start.4
  1.3 0.0 copy-start.5
  1.3 0.0 copy-start.6
  1.3 0.0 copy-start.1
  1.3 0.0 copy-start.2
  1.3 0.0 copy-start.3
  1.3 82.9 %shard_map.180 = (bf16[256,2048]{1,0:T(8,128)(2,1)}, f32[1,16,2048]{2,1,0:T(8,128)}, f32[1,16,256]{2,1,0:T(8,128)}) custom-call(s32[16]{0:T(128)} %ids_any.1, s32[1]{0:T(128)S(6)} %copy.21.live_any, s32[8]{0:T(128)} %owner_any.1, bf16[256,2048]{1,0:T(8,128)(2,1)} %x_any.1, bf16[256,256]{1,0:T(8,128)(2,1)} %dv_any.1, s32[1024,256]{1,0:T(8,128)} %code_any.1, ...), custom_call_target="tpu_custom_call" | custom-call | tf_op jit(solution)/shard_map/pallas_call | solution.py:620
  84.3 0.0 copy-start
  84.3 0.0 copy-done.4
  84.3 0.0 copy-done.5
  84.3 0.0 copy-done.6
  84.3 1.4 %multiply_subtract_fusion.1 = (f32[1,16,256]{2,1,0:T(8,128)}, f32[1,16,256]{2,1,0:T(8,128)}, f32[1,16,256]{2,1,0:T(8,128)}) fusion(f32[1,16,256]{2,1,0:T(8,128)S(1)} %copy-done.4, f32[1,16,256]{2,1,0:T(8,128)} %get-tuple-element.12, f32[1,16,256]{2,1,0:T(8,128)S(1)} %copy-done.5, f32[1,16,256]{2,1,0:T(8,128)S(1)} %copy-done.6), kind=kLoop, calls=%fused_computation.6 | loop fusion | flops 61440 | bytes 114688 | tf_op jit(solution)/shard_map/sub | solution.py:47
  85.8 0.0 copy-done.1
  85.8 0.0 copy-done.2
  85.8 0.0 copy-done.3
  85.8 1.7 %multiply_subtract_fusion = (f32[1,16,2048]{2,1,0:T(8,128)}, f32[1,16,2048]{2,1,0:T(8,128)}, f32[1,16,2048]{2,1,0:T(8,128)}) fusion(f32[1,16,2048]{2,1,0:T(8,128)S(1)} %copy-done.1, f32[1,16,2048]{2,1,0:T(8,128)} %get-tuple-element.11, f32[1,16,2048]{2,1,0:T(8,128)S(1)} %copy-done.2, f32[1,16,2048]{2,1,0:T(8,128)S(1)} %copy-done.3), kind=kLoop, calls=%fused_computation.2 | loop fusion | flops 491520 | bytes 917504 | tf_op jit(solution)/shard_map/sub | solution.py:47
  87.5 0.0 copy-done
  87.5 1.0 %copy.22 = bf16[256,2048]{1,0:T(8,128)(2,1)} copy(bf16[256,2048]{1,0:T(8,128)(2,1)S(1)} %copy-done) | data formatting | bytes 2097152
Async XLA Ops:
  1.3 83.0 %copy-start.4 = (f32[1,16,256]{2,1,0:T(8,128)S(1)}, f32[1,16,256]{2,1,0:T(8,128)}, u32[]{:S(2)}) copy-start(f32[1,16,256]{2,1,0:T(8,128)} %fu_any.1) | copy-start | bytes 49156
  1.3 83.0 %copy-start.5 = (f32[1,16,256]{2,1,0:T(8,128)S(1)}, f32[1,16,256]{2,1,0:T(8,128)}, u32[]{:S(2)}) copy-start(f32[1,16,256]{2,1,0:T(8,128)} %param.24) | copy-start | bytes 49156
  1.3 83.0 %copy-start.6 = (f32[1,16,256]{2,1,0:T(8,128)S(1)}, f32[1,16,256]{2,1,0:T(8,128)}, u32[]{:S(2)}) copy-start(f32[1,16,256]{2,1,0:T(8,128)} %param.25) | copy-start | bytes 49156
  1.3 84.5 %copy-start.1 = (f32[1,16,2048]{2,1,0:T(8,128)S(1)}, f32[1,16,2048]{2,1,0:T(8,128)}, u32[]{:S(2)}) copy-start(f32[1,16,2048]{2,1,0:T(8,128)} %fd_any.1) | copy-start | bytes 393220
  1.3 84.5 %copy-start.2 = (f32[1,16,2048]{2,1,0:T(8,128)S(1)}, f32[1,16,2048]{2,1,0:T(8,128)}, u32[]{:S(2)}) copy-start(f32[1,16,2048]{2,1,0:T(8,128)} %param.22) | copy-start | bytes 393220
  1.3 84.4 %copy-start.3 = (f32[1,16,2048]{2,1,0:T(8,128)S(1)}, f32[1,16,2048]{2,1,0:T(8,128)}, u32[]{:S(2)}) copy-start(f32[1,16,2048]{2,1,0:T(8,128)} %param.23) | copy-start | bytes 393220
  84.3 3.2 %copy-start = (bf16[256,2048]{1,0:T(8,128)(2,1)S(1)}, bf16[256,2048]{1,0:T(8,128)(2,1)}, u32[]{:S(2)}) copy-start(bf16[256,2048]{1,0:T(8,128)(2,1)} %get-tuple-element.26) | copy-start | bytes 3145732

commit v3 on v2

--- a/solution.py
+++ b/solution.py
@@ -223,8 +223,10 @@
     gy_r,
     gz_s,
     gz_r,
-    dv_s,
-    dvf_s,
+    dvz_s,
+    dvy_s,
+    dvx_s,
+    dvc_s,
     dv_r,
     part_s,
     part_r,
@@ -239,11 +241,12 @@
     t = lax.axis_index("tensor")
     z, y = f // 2, f % 2
     x, c = t // 2, t % 2
-    planes, wide = fsdp // 2, tensor // 2
+    pair, odd = z // 2, z % 2
+    wide, planes = tensor // 2, fsdp // 2
     tok_rows, width = x_ref.shape
     value = dv_ref.shape[1]
     w_rows = code_ref.shape[0]
-    step_rows = w_rows // CHUNKS
+    step_rows = w_rows // (2 * CHUNKS)
     rank = fd_ref.shape[1]
     slots = ids_ref.shape[0]
     seq = tok_rows // slots
@@ -287,30 +290,24 @@
         pending.append((copy, cond))
 
     barrier = pltpu.get_barrier_semaphore()
-    chips = [(dx, dy) for dx in range(wide) for dy in range(2)]
-    greeted = 0
-    for step in range(1, fsdp):
+    greeted = []
+
+    def greet(df, dt):
         pl.semaphore_signal(
             barrier,
             inc=1,
-            device_id={"fsdp": (f + step) % fsdp, "tensor": t},
+            device_id={"fsdp": df, "tensor": dt},
             device_id_type=pl.DeviceIdType.MESH,
         )
-        greeted += 1
-    for dx, dy in chips:
-        for dc in range(2):
-            if dx == 0 and dc == 0:
-                continue
-            pl.semaphore_signal(
-                barrier,
-                inc=1,
-                device_id={
-                    "fsdp": 2 * z + (y + dy) % 2,
-                    "tensor": 2 * ((x + dx) % wide) + (c + dc) % 2,
-                },
-                device_id_type=pl.DeviceIdType.MESH,
-            )
-            greeted += 1
+        greeted.append(1)
+
+    for n in range(1, 8):
+        near = 2 * pair + (odd + n // 4) % 2
+        greet(2 * near + (y + n // 2) % 2, 2 * x + (c + n) % 2)
+    for d in range(1, wide):
+        for e in range(2):
+            greet(2 * (2 * ((pair + d) % wide) + e) + y, t)
+            greet(f, 2 * ((x + d) % wide) + e)
 
     loads["fd"].wait()
     loads["fu"].wait()
@@ -322,10 +319,10 @@
     masked = jnp.where(
         tok_index < live_ref[0] * seq, dv_ref[...].astype(jnp.float32), 0.0
     ).astype(jnp.bfloat16)
-    dvs[t, y] = masked
-
-    def dequant(chunk):
-        rows = pl.ds(chunk * step_rows, step_rows)
+    dvs[t, odd, y] = masked
+
+    def dequant(half, chunk):
+        rows = pl.ds((half * CHUNKS + chunk) * step_rows, step_rows)
         levels = level_tree(code_ref[rows, :])
         scales = jnp.transpose(scale_ref[:, rows])
         blocks = scales.shape[1]
@@ -334,9 +331,9 @@
         spread = jnp.broadcast_to(scales[:, blocks - 1 : blocks], (step_rows, value))
         for n in reversed(range(blocks - 1)):
             spread = jnp.where(lane < (n + 1) * block, scales[:, n : n + 1], spread)
-        col[z, rows, :] = (levels * spread).astype(jnp.bfloat16)
-
-    pl.semaphore_wait(barrier, greeted)
+        col[pair, half, chunk] = (levels * spread).astype(jnp.bfloat16)
+
+    pl.semaphore_wait(barrier, len(greeted))
 
     def fac_copy(dz, source):
         return remote(
@@ -352,91 +349,79 @@
         send(fac_copy(dz, f))
     send(fac_forward(0, f))
 
-    across = remote(
-        dvs.at[t, y], dvs.at[t, y], dv_s.at[0], dv_r.at[t, y], 2 * z + 1 - y, t
-    )
-    across_in = remote(
-        dvs.at[t, 1 - y], dvs.at[t, 1 - y], dv_s.at[0], dv_r.at[t, 1 - y], 2 * z + 1 - y, t
-    )
-    send(across)
-
-    def dv_copy(dx, st):
+    def dv_near(parity, sy):
+        ref = dvs.at[t, parity, sy]
+        return remote(ref, ref, dvz_s.at[0], dv_r.at[t, parity, sy], 2 * (4 * pair + 1 - z) + y, t)
+
+    def dv_over(n, parity, sy):
+        ref = dvs.at[t, parity, sy]
+        return remote(ref, ref, dvy_s.at[n], dv_r.at[t, parity, sy], 2 * z + 1 - y, t)
+
+    def dv_along(n, d, st, parity):
+        ref = dvs.at[st, parity]
+        to = 2 * ((x + d) % wide) + c
+        return remote(ref, ref, dvx_s.at[n, d], dv_r.at[st, parity, 0], f, to)
+
+    def dv_core(n, d, st, parity):
+        ref = dvs.at[st, parity]
+        return remote(ref, ref, dvc_s.at[n, d], dv_r.at[st, parity, 0], f, 2 * x + 1 - c)
+
+    def dv_share(n, parity):
+        dv_over(n, parity, 1 - y).wait_recv()
+        for d in range(1, wide):
+            send(dv_along(n, d, t, parity))
+        send(dv_core(n, 0, t, parity))
+
+    send(dv_over(0, odd, y))
+    send(dv_near(odd, y))
+
+    def col_copy(d, source, half, chunk):
+        ref = col.at[source, half, chunk]
         return remote(
-            dvs.at[st],
-            dvs.at[st],
-            dv_s.at[dx],
-            dv_r.at[st, 0],
+            ref,
+            ref,
+            col_s.at[d, half, chunk],
+            col_r.at[source, half, chunk],
+            2 * (2 * ((pair + d) % wide) + odd) + y,
+            t,
+        )
+
+    def wgt_copy(d, source, half, chunk):
+        return remote(
+            col.at[source, half, chunk],
+            wgt.at[t, chunk],
+            wgt_s.at[d, half, chunk],
+            wgt_r.at[t, chunk],
             f,
-            2 * ((x + dx) % wide) + c,
-        )
-
-    def dv_forward(dx, st):
-        return remote(dvs.at[st], dvs.at[st], dvf_s.at[dx], dv_r.at[st, 0], f, 2 * x + 1 - c)
-
-    def col_copy(way, p, chunk):
-        rows = pl.ds(chunk * step_rows, step_rows)
-        return remote(
-            col.at[p, rows, :],
-            col.at[p, rows, :],
-            col_s.at[way, p, chunk],
-            col_r.at[p, chunk],
-            f + (2 if way == 0 else -2),
-            t,
-        )
-
-    def in_plane(p, chunk, valid):
-        rows = pl.ds(chunk * step_rows, step_rows)
-        df, dt = 2 * z + p % 2, 2 * (p // 2) + y
-        stays = jnp.logical_and(df == f, dt == t)
-
-        @pl.when(jnp.logical_and(valid, stays))
-        def _():
-            wgt[t, rows, :] = col[p, rows, :]
-
-        copy = remote(
-            col.at[p, rows, :],
-            wgt.at[t, rows, :],
-            wgt_s.at[p, chunk],
-            wgt_r.at[t, chunk],
-            df,
-            dt,
-        )
-        send(copy, jnp.logical_and(valid, jnp.logical_not(stays)))
-
-    def own(chunk):
-        send(col_copy(0, z, chunk), z < planes - 1)
-        send(col_copy(1, z, chunk), z > 0)
-        in_plane(z, chunk, z >= 0)
-
-    def relay(step):
-        for s in range(1, planes):
-            chunk = step - s
-            if chunk < 0 or chunk >= CHUNKS:
-                continue
-            for way in range(2):
-                p = z - s if way == 0 else z + s
-                valid = p >= 0 if way == 0 else p < planes
-                further = z < planes - 1 if way == 0 else z > 0
-                held = jnp.clip(p, 0, planes - 1)
-                pl.when(valid)(col_copy(way, held, chunk).wait_recv)
-                send(col_copy(way, held, chunk), jnp.logical_and(valid, further))
-                in_plane(held, chunk, valid)
+            2 * source + half,
+        )
+
+    def hand_out(d, half, chunk):
+        source = (pair + d) % wide
+        send(wgt_copy(d, source, half, chunk), 2 * source + half != t)
 
     loads["scale"].wait()
     loads["code"].wait()
     for chunk in range(CHUNKS):
-        dequant(chunk)
-        own(chunk)
+        for half in range(2):
+            dequant(half, chunk)
+            for d in range(1, wide):
+                send(col_copy(d, pair, half, chunk))
+            hand_out(0, half, chunk)
+
+    def forward(chunk):
+        for d in range(1, wide):
+            for half in range(2):
+                col_copy(d, (pair + d) % wide, half, chunk).wait_recv()
+                hand_out(d, half, chunk)
 
     for dz in range(1, planes):
         source = (f + 2 * dz) % fsdp
         fac_copy(dz, source).wait_recv()
         send(fac_forward(dz, source))
-    across_in.wait_recv()
-    for dx in range(1, wide):
-        send(dv_copy(dx, t))
-    send(dv_forward(0, t))
-    relay(1)
+    dv_share(0, odd)
+    dv_near(1 - odd, y).wait_recv()
+    send(dv_over(1, 1 - odd, y))
 
     loads["ids"].wait()
     loads["owner"].wait()
@@ -450,7 +435,7 @@
     named = lax.broadcasted_iota(jnp.int32, (flat, tok_rows), 0) // rank
     chosen = named == jnp.broadcast_to(slot_row, (flat, tok_rows))
 
-    relay(2)
+    forward(0)
     for dz in range(planes):
         source = (2 * z + 2 * dz) % fsdp + 1 - y
         fac_forward(dz, source).wait_recv()
@@ -471,11 +456,8 @@
     for step in range(1, tensor):
         send(part_copy((t + step) % tensor, t))
 
-    relay(3)
-    for dx in range(1, wide):
-        st = 2 * ((x + dx) % wide) + c
-        dv_copy(dx, st).wait_recv()
-        send(dv_forward(dx, st))
+    dv_share(1, 1 - odd)
+    forward(1)
 
     for step in range(1, tensor):
         source = (t + step) % tensor
@@ -504,86 +486,96 @@
             gz.at[to], grecv.at[source], gz_s.at[dz], gz_r.at[source], (f + 2 * dz) % fsdp, t
         )
 
-    relay(4)
-    for st in range(tensor):
-        pl.when(st % 2 != c)(dv_forward(0, st).wait_recv)
-
-    def multiply(chunk):
-        rows = pl.ds(chunk * step_rows, step_rows)
-        for st in range(tensor):
-            stays = jnp.logical_and(c == y, t == st)
-            arrived = remote(
-                col.at[0, rows, :],
-                wgt.at[st, rows, :],
-                wgt_s.at[0, chunk],
-                wgt_r.at[st, chunk],
-                f,
-                t,
-            )
-            pl.when(jnp.logical_not(stays))(arrived.wait_recv)
-        for half in range(2):
-            total = right_product(dvs[0, half], wgt[0, rows, :])
-            for st in range(1, tensor):
-                total = total + right_product(dvs[st, half], wgt[st, rows, :])
-            outs[half, chunk] = total.astype(jnp.bfloat16)
-            df, dt = 2 * z + half, 2 * x + y
-            stays = jnp.logical_and(df == f, dt == t)
-
-            @pl.when(stays)
-            def _():
-                base[c, chunk] = outs[half, chunk]
-
-            copy = remote(
-                outs.at[half, chunk],
-                base.at[c, chunk],
-                out_s.at[half, chunk],
-                out_r.at[c, chunk],
-                df,
-                dt,
-            )
-            send(copy, jnp.logical_not(stays))
-
-    multiply(0)
+    forward(2)
+    for n, parity in enumerate((odd, 1 - odd)):
+        for d in range(1, wide):
+            st = 2 * ((x + d) % wide) + c
+            dv_along(n, d, st, parity).wait_recv()
+            send(dv_core(n, d, st, parity))
     over.wait_recv()
     gz[...] = (gsend[y].astype(jnp.float32) + gy[...].astype(jnp.float32)).astype(jnp.bfloat16)
     for dz in range(1, planes):
         send(grad_copy(dz, (z + dz) % planes, z))
     grecv[pl.ds(z, 1)] = gz[pl.ds(z, 1)]
-
-    for step in range(5, CHUNKS + planes):
-        relay(step)
-        if step - planes < CHUNKS - 1:
-            multiply(step - planes)
+    for later in range(3, CHUNKS):
+        forward(later)
+
+    for d in range(wide):
+        for parity in range(2):
+            dv_core(0, 0, 2 * d + 1 - c, parity).wait_recv()
+
+    def multiply(chunk):
+        for step in range(1, tensor):
+            source = (t + step) % tensor
+            arrived = remote(
+                col.at[0, 0, chunk],
+                wgt.at[source, chunk],
+                wgt_s.at[0, 0, chunk],
+                wgt_r.at[source, chunk],
+                f,
+                source,
+            )
+            arrived.wait_recv()
+        rows = 4 * tok_rows
+        total = right_product(dvs[t].reshape(rows, value), col[x, c, chunk])
+        for step in range(1, tensor):
+            source = (t + step) % tensor
+            total = total + right_product(dvs[source].reshape(rows, value), wgt[source, chunk])
+        for parity in range(2):
+            for half in range(2):
+                start = (2 * parity + half) * tok_rows
+                piece = total[start : start + tok_rows].astype(jnp.bfloat16)
+                outs[chunk, parity, half] = piece
+                df, dt = 2 * (2 * pair + parity) + half, 2 * x + odd
+                stays = jnp.logical_and(df == f, dt == t)
+
+                @pl.when(stays)
+                def _(piece=piece):
+                    base[y, c, chunk] = piece
+
+                copy = remote(
+                    outs.at[chunk, parity, half],
+                    base.at[y, c, chunk],
+                    out_s.at[chunk, parity, half],
+                    out_r.at[y, c, chunk],
+                    df,
+                    dt,
+                )
+                send(copy, jnp.logical_not(stays))
+
+    for chunk in range(CHUNKS):
+        multiply(chunk)
+
     for dz in range(1, planes):
         grad_copy(dz, 0, (z + dz) % planes).wait_recv()
     dg_ref[...] = jnp.sum(grecv[:, :, 0:width].astype(jnp.float32), axis=0, keepdims=True)
     ug_ref[...] = jnp.sum(
         grecv[:, :, width : width + value].astype(jnp.float32), axis=0, keepdims=True
     )
-    multiply(CHUNKS - 1)
 
     for chunk in range(CHUNKS):
         for half in range(2):
-            stays = jnp.logical_and(half == c, c == f % 2)
-            arrived = remote(
-                outs.at[0, chunk],
-                base.at[half, chunk],
-                out_s.at[0, chunk],
-                out_r.at[half, chunk],
-                f,
-                t,
-            )
-            pl.when(jnp.logical_not(stays))(arrived.wait_recv)
-            start = half * w_rows + chunk * step_rows
-            low_term = lax.dot_general(
-                grad_spread,
-                fac[:, :, start : start + step_rows].reshape(flat, step_rows),
-                (((0,), (0,)), ((), ())),
-                preferred_element_type=jnp.float32,
-            )
-            out_ref[:, start : start + step_rows] = (
-                base[half, chunk].astype(jnp.float32) + low_term * inverse_width
-            ).astype(jnp.bfloat16)
+            for core in range(2):
+                stays = jnp.logical_and(odd == c, jnp.logical_and(half == y, core == c))
+                arrived = remote(
+                    outs.at[chunk, 0, 0],
+                    base.at[half, core, chunk],
+                    out_s.at[chunk, 0, 0],
+                    out_r.at[half, core, chunk],
+                    f,
+                    2 * x + 1 - c,
+                )
+                pl.when(jnp.logical_not(stays))(arrived.wait_recv)
+                start = half * w_rows + (core * CHUNKS + chunk) * step_rows
+                low_term = lax.dot_general(
+                    grad_spread,
+                    fac[:, :, start : start + step_rows].reshape(flat, step_rows),
+                    (((0,), (0,)), ((), ())),
+                    preferred_element_type=jnp.float32,
+                )
+                out_ref[:, start : start + step_rows] = (
+                    base[half, core, chunk].astype(jnp.float32) + low_term * inverse_width
+                ).astype(jnp.bfloat16)
 
     for copy, cond in pending:
         if cond is None:
@@ -612,7 +604,8 @@
     value = value_grad.shape[1]
     w_rows = quant_codes.shape[0]
     rank = factor_down.shape[1]
-    step_rows = w_rows // CHUNKS
+    step_rows = w_rows // (2 * CHUNKS)
+    wide, planes = tensor // 2, fsdp // 2
     low = jnp.bfloat16
     dma = pltpu.SemaphoreType.DMA
     vmem = pl.BlockSpec(memory_space=pltpu.VMEM)
@@ -638,34 +631,36 @@
             pltpu.VMEM(factor_up.shape, jnp.float32),
             dma((9,)),
             pltpu.VMEM((fsdp, rank, width + value), low),
-            pltpu.VMEM((2, fsdp // 2, rank, width + value), low),
-            pltpu.VMEM((fsdp // 2, rank, width + value), low),
-            pltpu.VMEM((fsdp // 2, rank, width + value), low),
-            pltpu.VMEM((fsdp // 2, rank, width + value), low),
-            pltpu.VMEM((tensor, 2, tok_rows, value), low),
+            pltpu.VMEM((2, planes, rank, width + value), low),
+            pltpu.VMEM((planes, rank, width + value), low),
+            pltpu.VMEM((planes, rank, width + value), low),
+            pltpu.VMEM((planes, rank, width + value), low),
+            pltpu.VMEM((tensor, 2, 2, tok_rows, value), low),
             pltpu.VMEM((tensor, 2 * rank, tok_rows), jnp.float32),
-            pltpu.VMEM((fsdp // 2, w_rows, value), low),
-            pltpu.VMEM((tensor, w_rows, value), low),
-            pltpu.VMEM((2, CHUNKS, tok_rows, step_rows), low),
-            pltpu.VMEM((2, CHUNKS, tok_rows, step_rows), low),
-            dma((fsdp // 2,)),
-            dma((fsdp // 2,)),
+            pltpu.VMEM((wide, 2, CHUNKS, step_rows, value), low),
+            pltpu.VMEM((tensor, CHUNKS, step_rows, value), low),
+            pltpu.VMEM((CHUNKS, 2, 2, tok_rows, step_rows), low),
+            pltpu.VMEM((2, 2, CHUNKS, tok_rows, step_rows), low),
+            dma((planes,)),
+            dma((planes,)),
             dma((fsdp,)),
             dma((1,)),
             dma((1,)),
-            dma((fsdp // 2,)),
-            dma((fsdp // 2,)),
-            dma((tensor // 2,)),
-            dma((tensor // 2,)),
-            dma((tensor, 2)),
+            dma((planes,)),
+            dma((planes,)),
+            dma((1,)),
+            dma((2,)),
+            dma((2, wide)),
+            dma((2, wide)),
+            dma((tensor, 2, 2)),
             dma((tensor,)),
             dma((tensor,)),
-            dma((2, fsdp // 2, CHUNKS)),
-            dma((fsdp // 2, CHUNKS)),
-            dma((fsdp // 2, CHUNKS)),
+            dma((wide, 2, CHUNKS)),
+            dma((wide, 2, CHUNKS)),
+            dma((wide, 2, CHUNKS)),
             dma((tensor, CHUNKS)),
-            dma((2, CHUNKS)),
-            dma((2, CHUNKS)),
+            dma((CHUNKS, 2, 2)),
+            dma((2, 2, CHUNKS)),
         ],
         compiler_params=pltpu.CompilerParams(
             collective_id=0, has_side_effects=True, vmem_limit_bytes=56 * 1024 * 1024

time: 88.7 us -> 69.5 us (0.78)
  the two profiles are of different devices: /device:TPU:6 before, /device:TPU:21 now
where the time goes in v3:
time: 69.5 us; the launch traced here: 69.2 us
  Pallas kernels  63.7 us (92%)
  other arithmetic  3.14 us (5%)
  between operations  1.38 us (2%)
  local copies, waits for them, and re-layouts  1 us (1%)
    pallas_call x1, Pallas kernels, fused(): pl.pallas_call(functools.partial(fused_kernel, fsdp, tensor), out_shape=(...  63.7 us
    sub x2, other arithmetic, adam_update(): new_param = param - learn_rate * (corrected / divisor + decay_rate * param)  3.14 us

profile of v3, /device:TPU:21, one launch (start us, length us, event | category | flops | bytes accessed | tf_op | source)
XLA Modules:
  0.0 69.2 jit_solution(4903566008208873126)
XLA Ops:
  1.3 0.0 copy-start.4
  1.3 0.0 copy-start.5
  1.3 0.0 copy-start.6
  1.3 0.0 copy-start.1
  1.3 0.0 copy-start.2
  1.3 0.0 copy-start.3
  1.3 63.7 %shard_map.180 = (bf16[256,2048]{1,0:T(8,128)(2,1)}, f32[1,16,2048]{2,1,0:T(8,128)}, f32[1,16,256]{2,1,0:T(8,128)}) custom-call(s32[16]{0:T(128)} %ids_any.1, s32[1]{0:T(128)S(6)} %copy.21.live_any, s32[8]{0:T(128)} %owner_any.1, bf16[256,2048]{1,0:T(8,128)(2,1)} %x_any.1, bf16[256,256]{1,0:T(8,128)(2,1)} %dv_any.1, s32[1024,256]{1,0:T(8,128)} %code_any.1, ...), custom_call_target="tpu_custom_call" | custom-call | tf_op jit(solution)/shard_map/pallas_call | solution.py:613
  65.0 0.0 copy-start
  65.1 0.0 copy-done.4
  65.1 0.0 copy-done.5
  65.1 0.0 copy-done.6
  65.1 1.4 %multiply_subtract_fusion.1 = (f32[1,16,256]{2,1,0:T(8,128)}, f32[1,16,256]{2,1,0:T(8,128)}, f32[1,16,256]{2,1,0:T(8,128)}) fusion(f32[1,16,256]{2,1,0:T(8,128)S(1)} %copy-done.4, f32[1,16,256]{2,1,0:T(8,128)} %get-tuple-element.12, f32[1,16,256]{2,1,0:T(8,128)S(1)} %copy-done.5, f32[1,16,256]{2,1,0:T(8,128)S(1)} %copy-done.6), kind=kLoop, calls=%fused_computation.6 | loop fusion | flops 61440 | bytes 114688 | tf_op jit(solution)/shard_map/sub | solution.py:47
  66.5 0.0 copy-done.1
  66.5 0.0 copy-done.2
  66.5 0.0 copy-done.3
  66.5 1.7 %multiply_subtract_fusion = (f32[1,16,2048]{2,1,0:T(8,128)}, f32[1,16,2048]{2,1,0:T(8,128)}, f32[1,16,2048]{2,1,0:T(8,128)}) fusion(f32[1,16,2048]{2,1,0:T(8,128)S(1)} %copy-done.1, f32[1,16,2048]{2,1,0:T(8,128)} %get-tuple-element.11, f32[1,16,2048]{2,1,0:T(8,128)S(1)} %copy-done.2, f32[1,16,2048]{2,1,0:T(8,128)S(1)} %copy-done.3), kind=kLoop, calls=%fused_computation.2 | loop fusion | flops 491520 | bytes 917504 | tf_op jit(solution)/shard_map/sub | solution.py:47
  68.2 0.0 copy-done
  68.2 1.0 %copy.22 = bf16[256,2048]{1,0:T(8,128)(2,1)} copy(bf16[256,2048]{1,0:T(8,128)(2,1)S(1)} %copy-done) | data formatting | bytes 2097152
Async XLA Ops:
  1.3 63.8 %copy-start.4 = (f32[1,16,256]{2,1,0:T(8,128)S(1)}, f32[1,16,256]{2,1,0:T(8,128)}, u32[]{:S(2)}) copy-start(f32[1,16,256]{2,1,0:T(8,128)} %fu_any.1) | copy-start | bytes 49156
  1.3 63.8 %copy-start.5 = (f32[1,16,256]{2,1,0:T(8,128)S(1)}, f32[1,16,256]{2,1,0:T(8,128)}, u32[]{:S(2)}) copy-start(f32[1,16,256]{2,1,0:T(8,128)} %param.24) | copy-start | bytes 49156
  1.3 63.8 %copy-start.6 = (f32[1,16,256]{2,1,0:T(8,128)S(1)}, f32[1,16,256]{2,1,0:T(8,128)}, u32[]{:S(2)}) copy-start(f32[1,16,256]{2,1,0:T(8,128)} %param.25) | copy-start | bytes 49156
  1.3 65.2 %copy-start.1 = (f32[1,16,2048]{2,1,0:T(8,128)S(1)}, f32[1,16,2048]{2,1,0:T(8,128)}, u32[]{:S(2)}) copy-start(f32[1,16,2048]{2,1,0:T(8,128)} %fd_any.1) | copy-start | bytes 393220
  1.3 65.2 %copy-start.2 = (f32[1,16,2048]{2,1,0:T(8,128)S(1)}, f32[1,16,2048]{2,1,0:T(8,128)}, u32[]{:S(2)}) copy-start(f32[1,16,2048]{2,1,0:T(8,128)} %param.22) | copy-start | bytes 393220
  1.3 65.2 %copy-start.3 = (f32[1,16,2048]{2,1,0:T(8,128)S(1)}, f32[1,16,2048]{2,1,0:T(8,128)}, u32[]{:S(2)}) copy-start(f32[1,16,2048]{2,1,0:T(8,128)} %param.23) | copy-start | bytes 393220
  65.0 3.2 %copy-start = (bf16[256,2048]{1,0:T(8,128)(2,1)S(1)}, bf16[256,2048]{1,0:T(8,128)(2,1)}, u32[]{:S(2)}) copy-start(bf16[256,2048]{1,0:T(8,128)(2,1)} %get-tuple-element.26) | copy-start | bytes 3145732

commit v4 on v3

--- a/solution.py
+++ b/solution.py
@@ -192,9 +192,17 @@
     scale_any,
     fd_any,
     fu_any,
+    md_any,
+    sd_any,
+    mu_any,
+    su_any,
     out_ref,
-    dg_ref,
-    ug_ref,
+    nd_ref,
+    nu_ref,
+    nmd_ref,
+    nsd_ref,
+    nmu_ref,
+    nsu_ref,
     ids_ref,
     live_ref,
     owner_ref,
@@ -204,6 +212,10 @@
     scale_ref,
     fd_ref,
     fu_ref,
+    md_ref,
+    sd_ref,
+    mu_ref,
+    su_ref,
     in_s,
     fac,
     gsend,
@@ -216,6 +228,7 @@
     wgt,
     outs,
     base,
+    lows,
     fac_s,
     fac_f,
     fac_r,
@@ -267,6 +280,10 @@
             ("x", x_any, x_ref),
             ("ids", ids_any, ids_ref),
             ("owner", owner_any, owner_ref),
+            ("md", md_any, md_ref),
+            ("sd", sd_any, sd_ref),
+            ("mu", mu_any, mu_ref),
+            ("su", su_any, su_ref),
         )
     ):
         loads[name] = pltpu.make_async_copy(src, dst, in_s.at[n])
@@ -480,26 +497,21 @@
         gsend[slot % 2, slot // 2, :, width : width + value] = up_slot[slot]
     over = remote(gsend.at[1 - y], gy, gy_s.at[0], gy_r.at[0], 2 * z + 1 - y, t)
     send(over)
+    lows[...] = inverse_width * lax.dot_general(
+        grad_spread, all_down, (((0,), (0,)), ((), ())), preferred_element_type=jnp.float32
+    )
 
     def grad_copy(dz, to, source):
         return remote(
             gz.at[to], grecv.at[source], gz_s.at[dz], gz_r.at[source], (f + 2 * dz) % fsdp, t
         )
 
-    forward(2)
     for n, parity in enumerate((odd, 1 - odd)):
         for d in range(1, wide):
             st = 2 * ((x + d) % wide) + c
             dv_along(n, d, st, parity).wait_recv()
             send(dv_core(n, d, st, parity))
-    over.wait_recv()
-    gz[...] = (gsend[y].astype(jnp.float32) + gy[...].astype(jnp.float32)).astype(jnp.bfloat16)
-    for dz in range(1, planes):
-        send(grad_copy(dz, (z + dz) % planes, z))
-    grecv[pl.ds(z, 1)] = gz[pl.ds(z, 1)]
-    for later in range(3, CHUNKS):
-        forward(later)
-
+    forward(2)
     for d in range(wide):
         for parity in range(2):
             dv_core(0, 0, 2 * d + 1 - c, parity).wait_recv()
@@ -543,14 +555,31 @@
                 )
                 send(copy, jnp.logical_not(stays))
 
-    for chunk in range(CHUNKS):
-        multiply(chunk)
+    multiply(0)
+    over.wait_recv()
+    gz[...] = (gsend[y].astype(jnp.float32) + gy[...].astype(jnp.float32)).astype(jnp.bfloat16)
+    for dz in range(1, planes):
+        send(grad_copy(dz, (z + dz) % planes, z))
+    grecv[pl.ds(z, 1)] = gz[pl.ds(z, 1)]
+    multiply(1)
+    multiply(2)
+    for later in range(3, CHUNKS):
+        forward(later)
+        multiply(later)
 
     for dz in range(1, planes):
         grad_copy(dz, 0, (z + dz) % planes).wait_recv()
-    dg_ref[...] = jnp.sum(grecv[:, :, 0:width].astype(jnp.float32), axis=0, keepdims=True)
-    ug_ref[...] = jnp.sum(
+    for name in ("md", "sd", "mu", "su"):
+        loads[name].wait()
+    down_grad = jnp.sum(grecv[:, :, 0:width].astype(jnp.float32), axis=0, keepdims=True)
+    up_grad = jnp.sum(
         grecv[:, :, width : width + value].astype(jnp.float32), axis=0, keepdims=True
+    )
+    nd_ref[...], nmd_ref[...], nsd_ref[...] = adam_update(
+        fd_ref[...], down_grad, md_ref[...], sd_ref[...]
+    )
+    nu_ref[...], nmu_ref[...], nsu_ref[...] = adam_update(
+        fu_ref[...], up_grad, mu_ref[...], su_ref[...]
     )
 
     for chunk in range(CHUNKS):
@@ -567,14 +596,9 @@
                 )
                 pl.when(jnp.logical_not(stays))(arrived.wait_recv)
                 start = half * w_rows + (core * CHUNKS + chunk) * step_rows
-                low_term = lax.dot_general(
-                    grad_spread,
-                    fac[:, :, start : start + step_rows].reshape(flat, step_rows),
-                    (((0,), (0,)), ((), ())),
-                    preferred_element_type=jnp.float32,
-                )
-                out_ref[:, start : start + step_rows] = (
-                    base[half, core, chunk].astype(jnp.float32) + low_term * inverse_width
+                stop = start + step_rows
+                out_ref[:, start:stop] = (
+                    base[half, core, chunk].astype(jnp.float32) + lows[:, start:stop]
                 ).astype(jnp.bfloat16)
 
     for copy, cond in pending:
@@ -582,6 +606,16 @@
             copy.wait_send()
         else:
             pl.when(cond)(copy.wait_send)
+
+
+def write_kernel(count, *refs):
+    copies = [
+        pltpu.make_async_copy(refs[n], refs[count + n], refs[2 * count].at[n]) for n in range(count)
+    ]
+    for copy in copies:
+        copy.start()
+    for copy in copies:
+        copy.wait()
 
 
 def fused(fsdp, tensor, *args):
@@ -610,15 +644,21 @@
     dma = pltpu.SemaphoreType.DMA
     vmem = pl.BlockSpec(memory_space=pltpu.VMEM)
     like = jax.ShapeDtypeStruct
-    layer_input_gradient, down_gradient, up_gradient = pl.pallas_call(
+    shapes = (
+        like(layer_input.shape, low),
+        like(factor_down.shape, jnp.float32),
+        like(factor_up.shape, jnp.float32),
+        like(factor_down.shape, jnp.float32),
+        like(factor_down.shape, jnp.float32),
+        like(factor_up.shape, jnp.float32),
+        like(factor_up.shape, jnp.float32),
+    )
+    anywhere = pl.BlockSpec(memory_space=pl.ANY)
+    results = pl.pallas_call(
         functools.partial(fused_kernel, fsdp, tensor),
-        out_shape=(
-            like(layer_input.shape, low),
-            like(factor_down.shape, jnp.float32),
-            like(factor_up.shape, jnp.float32),
-        ),
-        in_specs=[pl.BlockSpec(memory_space=pl.ANY)] * 9,
-        out_specs=(vmem,) * 3,
+        out_shape=shapes,
+        in_specs=[anywhere] * 13,
+        out_specs=(vmem,) * 7,
         scratch_shapes=[
             pltpu.SMEM(tenant_ids.shape, jnp.int32),
             pltpu.SMEM(live_counts.shape, jnp.int32),
@@ -629,7 +669,11 @@
             pltpu.VMEM(block_scales.shape[::-1], jnp.float32),
             pltpu.VMEM(factor_down.shape, jnp.float32),
             pltpu.VMEM(factor_up.shape, jnp.float32),
-            dma((9,)),
+            pltpu.VMEM(moment_down.shape, jnp.float32),
+            pltpu.VMEM(second_down.shape, jnp.float32),
+            pltpu.VMEM(moment_up.shape, jnp.float32),
+            pltpu.VMEM(second_up.shape, jnp.float32),
+            dma((13,)),
             pltpu.VMEM((fsdp, rank, width + value), low),
             pltpu.VMEM((2, planes, rank, width + value), low),
             pltpu.VMEM((planes, rank, width + value), low),
@@ -641,6 +685,7 @@
             pltpu.VMEM((tensor, CHUNKS, step_rows, value), low),
             pltpu.VMEM((CHUNKS, 2, 2, tok_rows, step_rows), low),
             pltpu.VMEM((2, 2, CHUNKS, tok_rows, step_rows), low),
+            pltpu.VMEM((tok_rows, width), jnp.float32),
             dma((planes,)),
             dma((planes,)),
             dma((fsdp,)),
@@ -663,7 +708,7 @@
             dma((2, 2, CHUNKS)),
         ],
         compiler_params=pltpu.CompilerParams(
-            collective_id=0, has_side_effects=True, vmem_limit_bytes=56 * 1024 * 1024
+            collective_id=0, has_side_effects=True, vmem_limit_bytes=60 * 1024 * 1024
         ),
     )(
         tenant_ids,
@@ -675,20 +720,19 @@
         block_scales.T,
         factor_down,
         factor_up,
-    )
-    new_down, new_moment_down, new_second_down = adam_update(
-        factor_down, down_gradient, moment_down, second_down
-    )
-    new_up, new_moment_up, new_second_up = adam_update(factor_up, up_gradient, moment_up, second_up)
-    return (
-        layer_input_gradient,
-        new_down,
-        new_up,
-        new_moment_down,
-        new_second_down,
-        new_moment_up,
-        new_second_up,
-    )
+        moment_down,
+        second_down,
+        moment_up,
+        second_up,
+    )
+    return pl.pallas_call(
+        functools.partial(write_kernel, len(shapes)),
+        out_shape=shapes,
+        in_specs=[anywhere] * len(shapes),
+        out_specs=(anywhere,) * len(shapes),
+        scratch_shapes=[dma((len(shapes),))],
+        compiler_params=pltpu.CompilerParams(vmem_limit_bytes=60 * 1024 * 1024),
+    )(*results)
 
 
 def solution(mesh):

time: 69.5 us -> 109 us (1.57)
  Pallas kernels: 63.7 us -> 107 us
  other arithmetic: 3.14 us -> 0 us
    pallas_call x1 -> x2, Pallas kernels: 63.7 us -> 107 us  [the longest x1 60.4 us: fused(): pl.pallas_call(functools.partial(fused_kernel, fsdp, tensor), out_shape=s...]
    sub x2 -> x0, other arithmetic: 3.14 us -> none  [adam_update(): new_param = param - learn_rate * (corrected / divisor + decay_rate * param)]
where the time goes in v4:
time: 109 us; the launch traced here: 108 us
  Pallas kernels  107 us (98%)
  between operations  1.29 us (1%)
    pallas_call x1, Pallas kernels, fused(): pl.pallas_call(functools.partial(fused_kernel, fsdp, tensor), out_shape=s...  60.4 us
    pallas_call x1, Pallas kernels, fused(): pl.pallas_call(functools.partial(write_kernel, len(shapes)), out_shape=sh...  46.3 us

profile of v4, /device:TPU:21, one launch (start us, length us, event | category | flops | bytes accessed | tf_op | source)
XLA Modules:
  0.0 108.0 jit_solution(8986987946844445762)
XLA Ops:
  1.3 60.4 %shard_map.180 = (bf16[256,2048]{1,0:T(8,128)(2,1)}, f32[1,16,2048]{2,1,0:T(8,128)}, f32[1,16,256]{2,1,0:T(8,128)}, f32[1,16,2048]{2,1,0:T(8,128)}, f32[1,16,204...) custom-call(s32[16]{0:T(128)} %ids_any.1, s32[1]{0:T(128)S(6)} %copy.20.live_any, s32[8]{0:T(128)} %owner_any.1, ...), custom_call_target="tpu_custom_call" | custom-call | tf_op jit(solution)/shard_map/pallas_call | solution.py:657
  61.7 46.3 %shard_map.181 = (bf16[256,2048]{1,0:T(8,128)(2,1)}, f32[1,16,2048]{2,1,0:T(8,128)}, f32[1,16,256]{2,1,0:T(8,128)}, f32[1,16,2048]{2,1,0:T(8,128)}, f32[1,16,204...) custom-call(bf16[256,2048]{1,0:T(8,128)(2,1)} %get-tuple-element.14.refs_0_, ...), custom_call_target="tpu_custom_call" | custom-call | tf_op jit(solution)/shard_map/pallas_call | solution.py:728

commit v5 on v4

--- a/solution.py
+++ b/solution.py
@@ -374,23 +374,23 @@
         ref = dvs.at[t, parity, sy]
         return remote(ref, ref, dvy_s.at[n], dv_r.at[t, parity, sy], 2 * z + 1 - y, t)
 
-    def dv_along(n, d, st, parity):
-        ref = dvs.at[st, parity]
+    def dv_along(n, d, st, parity, sy):
+        ref = dvs.at[st, parity, sy]
         to = 2 * ((x + d) % wide) + c
-        return remote(ref, ref, dvx_s.at[n, d], dv_r.at[st, parity, 0], f, to)
-
-    def dv_core(n, d, st, parity):
-        ref = dvs.at[st, parity]
-        return remote(ref, ref, dvc_s.at[n, d], dv_r.at[st, parity, 0], f, 2 * x + 1 - c)
-
-    def dv_share(n, parity):
-        dv_over(n, parity, 1 - y).wait_recv()
+        return remote(ref, ref, dvx_s.at[n, d], dv_r.at[st, parity, sy], f, to)
+
+    def dv_core(n, d, st, parity, sy):
+        ref = dvs.at[st, parity, sy]
+        return remote(ref, ref, dvc_s.at[n, d], dv_r.at[st, parity, sy], f, 2 * x + 1 - c)
+
+    def dv_share(n, parity, sy):
         for d in range(1, wide):
-            send(dv_along(n, d, t, parity))
-        send(dv_core(n, 0, t, parity))
-
+            send(dv_along(n, d, t, parity, sy))
+        send(dv_core(n, 0, t, parity, sy))
+
+    send(dv_near(odd, y))
     send(dv_over(0, odd, y))
-    send(dv_near(odd, y))
+    dv_share(0, odd, y)
 
     def col_copy(d, source, half, chunk):
         ref = col.at[source, half, chunk]
@@ -424,7 +424,6 @@
             dequant(half, chunk)
             for d in range(1, wide):
                 send(col_copy(d, pair, half, chunk))
-            hand_out(0, half, chunk)
 
     def forward(chunk):
         for d in range(1, wide):
@@ -432,13 +431,25 @@
                 col_copy(d, (pair + d) % wide, half, chunk).wait_recv()
                 hand_out(d, half, chunk)
 
+    def give(chunk):
+        for half in range(2):
+            hand_out(0, half, chunk)
+
+    give(0)
+    dv_over(0, odd, 1 - y).wait_recv()
+    dv_share(1, odd, 1 - y)
     for dz in range(1, planes):
         source = (f + 2 * dz) % fsdp
         fac_copy(dz, source).wait_recv()
         send(fac_forward(dz, source))
-    dv_share(0, odd)
     dv_near(1 - odd, y).wait_recv()
     send(dv_over(1, 1 - odd, y))
+    dv_share(2, 1 - odd, y)
+    give(1)
+    dv_over(1, 1 - odd, 1 - y).wait_recv()
+    dv_share(3, 1 - odd, 1 - y)
+    for later in range(2, CHUNKS):
+        give(later)
 
     loads["ids"].wait()
     loads["owner"].wait()
@@ -473,48 +484,19 @@
     for step in range(1, tensor):
         send(part_copy((t + step) % tensor, t))
 
-    dv_share(1, 1 - odd)
-    forward(1)
-
-    for step in range(1, tensor):
-        source = (t + step) % tensor
-        part_copy(source, source).wait_recv()
-    sums = jnp.sum(part[...], axis=0)
-    low = sums.astype(jnp.bfloat16).astype(jnp.float32)
-
-    def spread_out(rows):
-        tiled = jnp.broadcast_to(rows[None], (fsdp, rank, tok_rows)).reshape(flat, tok_rows)
-        return jnp.where(chosen, tiled, 0.0).astype(jnp.bfloat16)
-
-    in_spread = spread_out(low[0:rank])
-    grad_spread = spread_out(low[rank : 2 * rank])
-    down_terms = jnp.dot(grad_spread, x_ref[...], preferred_element_type=jnp.float32)
-    by_slot = (down_terms * inverse_width).astype(jnp.bfloat16).reshape(fsdp, rank, width)
-    up_terms = jnp.dot(in_spread, masked, preferred_element_type=jnp.float32)
-    up_slot = (up_terms * coefficient).astype(jnp.bfloat16).reshape(fsdp, rank, value)
-    for slot in range(fsdp):
-        gsend[slot % 2, slot // 2, :, 0:width] = by_slot[slot]
-        gsend[slot % 2, slot // 2, :, width : width + value] = up_slot[slot]
-    over = remote(gsend.at[1 - y], gy, gy_s.at[0], gy_r.at[0], 2 * z + 1 - y, t)
-    send(over)
-    lows[...] = inverse_width * lax.dot_general(
-        grad_spread, all_down, (((0,), (0,)), ((), ())), preferred_element_type=jnp.float32
-    )
-
-    def grad_copy(dz, to, source):
-        return remote(
-            gz.at[to], grecv.at[source], gz_s.at[dz], gz_r.at[source], (f + 2 * dz) % fsdp, t
-        )
-
-    for n, parity in enumerate((odd, 1 - odd)):
+    for n, (parity, sy) in enumerate(
+        ((odd, y), (odd, 1 - y), (1 - odd, y), (1 - odd, 1 - y))
+    ):
         for d in range(1, wide):
             st = 2 * ((x + d) % wide) + c
-            dv_along(n, d, st, parity).wait_recv()
-            send(dv_core(n, d, st, parity))
-    forward(2)
+            dv_along(n, d, st, parity, sy).wait_recv()
+            send(dv_core(n, d, st, parity, sy))
+    forward(1)
+
     for d in range(wide):
         for parity in range(2):
-            dv_core(0, 0, 2 * d + 1 - c, parity).wait_recv()
+            for sy in range(2):
+                dv_core(0, 0, 2 * d + 1 - c, parity, sy).wait_recv()
 
     def multiply(chunk):
         for step in range(1, tensor):
@@ -556,13 +538,45 @@
                 send(copy, jnp.logical_not(stays))
 
     multiply(0)
+
+    for step in range(1, tensor):
+        source = (t + step) % tensor
+        part_copy(source, source).wait_recv()
+    sums = jnp.sum(part[...], axis=0)
+    low = sums.astype(jnp.bfloat16).astype(jnp.float32)
+
+    def spread_out(rows):
+        tiled = jnp.broadcast_to(rows[None], (fsdp, rank, tok_rows)).reshape(flat, tok_rows)
+        return jnp.where(chosen, tiled, 0.0).astype(jnp.bfloat16)
+
+    in_spread = spread_out(low[0:rank])
+    grad_spread = spread_out(low[rank : 2 * rank])
+    down_terms = jnp.dot(grad_spread, x_ref[...], preferred_element_type=jnp.float32)
+    by_slot = (down_terms * inverse_width).astype(jnp.bfloat16).reshape(fsdp, rank, width)
+    up_terms = jnp.dot(in_spread, masked, preferred_element_type=jnp.float32)
+    up_slot = (up_terms * coefficient).astype(jnp.bfloat16).reshape(fsdp, rank, value)
+    for slot in range(fsdp):
+        gsend[slot % 2, slot // 2, :, 0:width] = by_slot[slot]
+        gsend[slot % 2, slot // 2, :, width : width + value] = up_slot[slot]
+    over = remote(gsend.at[1 - y], gy, gy_s.at[0], gy_r.at[0], 2 * z + 1 - y, t)
+    send(over)
+
+    def grad_copy(dz, to, source):
+        return remote(
+            gz.at[to], grecv.at[source], gz_s.at[dz], gz_r.at[source], (f + 2 * dz) % fsdp, t
+        )
+
+    multiply(1)
+    forward(2)
     over.wait_recv()
     gz[...] = (gsend[y].astype(jnp.float32) + gy[...].astype(jnp.float32)).astype(jnp.bfloat16)
     for dz in range(1, planes):
         send(grad_copy(dz, (z + dz) % planes, z))
     grecv[pl.ds(z, 1)] = gz[pl.ds(z, 1)]
-    multiply(1)
     multiply(2)
+    lows[...] = inverse_width * lax.dot_general(
+        grad_spread, all_down, (((0,), (0,)), ((), ())), preferred_element_type=jnp.float32
+    )
     for later in range(3, CHUNKS):
         forward(later)
         multiply(later)
@@ -609,13 +623,16 @@
 
 
 def write_kernel(count, *refs):
-    copies = [
-        pltpu.make_async_copy(refs[n], refs[count + n], refs[2 * count].at[n]) for n in range(count)
-    ]
-    for copy in copies:
-        copy.start()
-    for copy in copies:
-        copy.wait()
+    held, sems = refs[2 * count : 3 * count], refs[3 * count]
+    loads = [pltpu.make_async_copy(refs[n], held[n], sems.at[0, n]) for n in range(count)]
+    stores = [pltpu.make_async_copy(held[n], refs[count + n], sems.at[1, n]) for n in range(count)]
+    for load in loads:
+        load.start()
+    for load, store in zip(loads, stores):
+        load.wait()
+        store.start()
+    for store in stores:
+        store.wait()
 
 
 def fused(fsdp, tensor, *args):
@@ -695,8 +712,8 @@
             dma((planes,)),
             dma((1,)),
             dma((2,)),
-            dma((2, wide)),
-            dma((2, wide)),
+            dma((4, wide)),
+            dma((4, wide)),
             dma((tensor, 2, 2)),
             dma((tensor,)),
             dma((tensor,)),
@@ -730,7 +747,7 @@
         out_shape=shapes,
         in_specs=[anywhere] * len(shapes),
         out_specs=(anywhere,) * len(shapes),
-        scratch_shapes=[dma((len(shapes),))],
+        scratch_shapes=[pltpu.VMEM(s.shape, s.dtype) for s in shapes] + [dma((2, len(shapes)))],
         compiler_params=pltpu.CompilerParams(vmem_limit_bytes=60 * 1024 * 1024),
     )(*results)
 

time: 109 us -> 62.6 us (0.57)
  Pallas kernels: 107 us -> 61.1 us
    pallas_call x1, Pallas kernels: 46.3 us -> 2.45 us  [fused(): pl.pallas_call(functools.partial(write_kernel, len(shapes)), out_shape=sh...]
    pallas_call x1, Pallas kernels: 60.4 us -> 58.7 us  [fused(): pl.pallas_call(functools.partial(fused_kernel, fsdp, tensor), out_shape=s...]
where the time goes in v5:
time: 62.6 us; the launch traced here: 62.4 us
  Pallas kernels  61.1 us (98%)
  between operations  1.29 us (2%)
    pallas_call x1, Pallas kernels, fused(): pl.pallas_call(functools.partial(fused_kernel, fsdp, tensor), out_shape=s...  58.7 us
    pallas_call x1, Pallas kernels, fused(): pl.pallas_call(functools.partial(write_kernel, len(shapes)), out_shape=sh...  2.45 us

profile of v5, /device:TPU:21, one launch (start us, length us, event | category | flops | bytes accessed | tf_op | source)
XLA Modules:
  0.0 62.4 jit_solution(5039641743356235284)
XLA Ops:
  1.3 58.7 %shard_map.180 = (bf16[256,2048]{1,0:T(8,128)(2,1)}, f32[1,16,2048]{2,1,0:T(8,128)}, f32[1,16,256]{2,1,0:T(8,128)}, f32[1,16,2048]{2,1,0:T(8,128)}, f32[1,16,204...) custom-call(s32[16]{0:T(128)} %ids_any.1, s32[1]{0:T(128)S(6)} %copy.20.live_any, s32[8]{0:T(128)} %owner_any.1, ...), custom_call_target="tpu_custom_call" | custom-call | tf_op jit(solution)/shard_map/pallas_call | solution.py:674
  59.9 2.4 %shard_map.181 = (bf16[256,2048]{1,0:T(8,128)(2,1)}, f32[1,16,2048]{2,1,0:T(8,128)}, f32[1,16,256]{2,1,0:T(8,128)}, f32[1,16,2048]{2,1,0:T(8,128)}, f32[1,16,204...) custom-call(bf16[256,2048]{1,0:T(8,128)(2,1)} %get-tuple-element.14.refs_0_, ...), custom_call_target="tpu_custom_call" | custom-call | tf_op jit(solution)/shard_map/pallas_call | solution.py:745

commit v6 on v5

--- a/solution.py
+++ b/solution.py
@@ -350,6 +350,10 @@
             spread = jnp.where(lane < (n + 1) * block, scales[:, n : n + 1], spread)
         col[pair, half, chunk] = (levels * spread).astype(jnp.bfloat16)
 
+    loads["scale"].wait()
+    loads["code"].wait()
+    dequant(0, 0)
+    dequant(1, 0)
     pl.semaphore_wait(barrier, len(greeted))
 
     def fac_copy(dz, source):
@@ -417,11 +421,10 @@
         source = (pair + d) % wide
         send(wgt_copy(d, source, half, chunk), 2 * source + half != t)
 
-    loads["scale"].wait()
-    loads["code"].wait()
     for chunk in range(CHUNKS):
         for half in range(2):
-            dequant(half, chunk)
+            if chunk > 0:
+                dequant(half, chunk)
             for d in range(1, wide):
                 send(col_copy(d, pair, half, chunk))
 
@@ -492,6 +495,33 @@
             dv_along(n, d, st, parity, sy).wait_recv()
             send(dv_core(n, d, st, parity, sy))
     forward(1)
+
+    for step in range(1, tensor):
+        source = (t + step) % tensor
+        part_copy(source, source).wait_recv()
+    sums = jnp.sum(part[...], axis=0)
+    low = sums.astype(jnp.bfloat16).astype(jnp.float32)
+
+    def spread_out(rows):
+        tiled = jnp.broadcast_to(rows[None], (fsdp, rank, tok_rows)).reshape(flat, tok_rows)
+        return jnp.where(chosen, tiled, 0.0).astype(jnp.bfloat16)
+
+    in_spread = spread_out(low[0:rank])
+    grad_spread = spread_out(low[rank : 2 * rank])
+    down_terms = jnp.dot(grad_spread, x_ref[...], preferred_element_type=jnp.float32)
+    by_slot = (down_terms * inverse_width).astype(jnp.bfloat16).reshape(fsdp, rank, width)
+    up_terms = jnp.dot(in_spread, masked, preferred_element_type=jnp.float32)
+    up_slot = (up_terms * coefficient).astype(jnp.bfloat16).reshape(fsdp, rank, value)
+    for slot in range(fsdp):
+        gsend[slot % 2, slot // 2, :, 0:width] = by_slot[slot]
+        gsend[slot % 2, slot // 2, :, width : width + value] = up_slot[slot]
+    over = remote(gsend.at[1 - y], gy, gy_s.at[0], gy_r.at[0], 2 * z + 1 - y, t)
+    send(over)
+
+    def grad_copy(dz, to, source):
+        return remote(
+            gz.at[to], grecv.at[source], gz_s.at[dz], gz_r.at[source], (f + 2 * dz) % fsdp, t
+        )
 
     for d in range(wide):
         for parity in range(2):
@@ -538,41 +568,13 @@
                 send(copy, jnp.logical_not(stays))
 
     multiply(0)
-
-    for step in range(1, tensor):
-        source = (t + step) % tensor
-        part_copy(source, source).wait_recv()
-    sums = jnp.sum(part[...], axis=0)
-    low = sums.astype(jnp.bfloat16).astype(jnp.float32)
-
-    def spread_out(rows):
-        tiled = jnp.broadcast_to(rows[None], (fsdp, rank, tok_rows)).reshape(flat, tok_rows)
-        return jnp.where(chosen, tiled, 0.0).astype(jnp.bfloat16)
-
-    in_spread = spread_out(low[0:rank])
-    grad_spread = spread_out(low[rank : 2 * rank])
-    down_terms = jnp.dot(grad_spread, x_ref[...], preferred_element_type=jnp.float32)
-    by_slot = (down_terms * inverse_width).astype(jnp.bfloat16).reshape(fsdp, rank, width)
-    up_terms = jnp.dot(in_spread, masked, preferred_element_type=jnp.float32)
-    up_slot = (up_terms * coefficient).astype(jnp.bfloat16).reshape(fsdp, rank, value)
-    for slot in range(fsdp):
-        gsend[slot % 2, slot // 2, :, 0:width] = by_slot[slot]
-        gsend[slot % 2, slot // 2, :, width : width + value] = up_slot[slot]
-    over = remote(gsend.at[1 - y], gy, gy_s.at[0], gy_r.at[0], 2 * z + 1 - y, t)
-    send(over)
-
-    def grad_copy(dz, to, source):
-        return remote(
-            gz.at[to], grecv.at[source], gz_s.at[dz], gz_r.at[source], (f + 2 * dz) % fsdp, t
-        )
-
-    multiply(1)
-    forward(2)
     over.wait_recv()
     gz[...] = (gsend[y].astype(jnp.float32) + gy[...].astype(jnp.float32)).astype(jnp.bfloat16)
     for dz in range(1, planes):
         send(grad_copy(dz, (z + dz) % planes, z))
     grecv[pl.ds(z, 1)] = gz[pl.ds(z, 1)]
+    multiply(1)
+    forward(2)
     multiply(2)
     lows[...] = inverse_width * lax.dot_general(
         grad_spread, all_down, (((0,), (0,)), ((), ())), preferred_element_type=jnp.float32
@@ -581,22 +583,7 @@
         forward(later)
         multiply(later)
 
-    for dz in range(1, planes):
-        grad_copy(dz, 0, (z + dz) % planes).wait_recv()
-    for name in ("md", "sd", "mu", "su"):
-        loads[name].wait()
-    down_grad = jnp.sum(grecv[:, :, 0:width].astype(jnp.float32), axis=0, keepdims=True)
-    up_grad = jnp.sum(
-        grecv[:, :, width : width + value].astype(jnp.float32), axis=0, keepdims=True
-    )
-    nd_ref[...], nmd_ref[...], nsd_ref[...] = adam_update(
-        fd_ref[...], down_grad, md_ref[...], sd_ref[...]
-    )
-    nu_ref[...], nmu_ref[...], nsu_ref[...] = adam_update(
-        fu_ref[...], up_grad, mu_ref[...], su_ref[...]
-    )
-
-    for chunk in range(CHUNKS):
+    def finish(chunk):
         for half in range(2):
             for core in range(2):
                 stays = jnp.logical_and(odd == c, jnp.logical_and(half == y, core == c))
@@ -614,6 +601,25 @@
                 out_ref[:, start:stop] = (
                     base[half, core, chunk].astype(jnp.float32) + lows[:, start:stop]
                 ).astype(jnp.bfloat16)
+
+    for chunk in range(CHUNKS - 1):
+        finish(chunk)
+    for dz in range(1, planes):
+        grad_copy(dz, 0, (z + dz) % planes).wait_recv()
+    for name in ("md", "sd", "mu", "su"):
+        loads[name].wait()
+    down_grad = jnp.sum(grecv[:, :, 0:width].astype(jnp.float32), axis=0, keepdims=True)
+    up_grad = jnp.sum(
+        grecv[:, :, width : width + value].astype(jnp.float32), axis=0, keepdims=True
+    )
+    nd_ref[...], nmd_ref[...], nsd_ref[...] = adam_update(
+        fd_ref[...], down_grad, md_ref[...], sd_ref[...]
+    )
+    nu_ref[...], nmu_ref[...], nsu_ref[...] = adam_update(
+        fu_ref[...], up_grad, mu_ref[...], su_ref[...]
+    )
+
+    finish(CHUNKS - 1)
 
     for copy, cond in pending:
         if cond is None:

time: 62.6 us -> 64.4 us (1.029)
  Pallas kernels: 61.1 us -> 62.9 us
    pallas_call x1, Pallas kernels: 58.7 us -> 60.5 us  [fused(): pl.pallas_call(functools.partial(fused_kernel, fsdp, tensor), out_shape=s...]
where the time goes in v6:
time: 64.4 us; the launch traced here: 64.2 us
  Pallas kernels  62.9 us (98%)
  between operations  1.29 us (2%)
    pallas_call x1, Pallas kernels, fused(): pl.pallas_call(functools.partial(fused_kernel, fsdp, tensor), out_shape=s...  60.5 us
    pallas_call x1, Pallas kernels, fused(): pl.pallas_call(functools.partial(write_kernel, len(shapes)), out_shape=sh...  2.45 us

profile of v6, /device:TPU:21, one launch (start us, length us, event | category | flops | bytes accessed | tf_op | source)
XLA Modules:
  0.0 64.2 jit_solution(5919769057351310207)
XLA Ops:
  1.3 60.5 %shard_map.180 = (bf16[256,2048]{1,0:T(8,128)(2,1)}, f32[1,16,2048]{2,1,0:T(8,128)}, f32[1,16,256]{2,1,0:T(8,128)}, f32[1,16,2048]{2,1,0:T(8,128)}, f32[1,16,204...) custom-call(s32[16]{0:T(128)} %ids_any.1, s32[1]{0:T(128)S(6)} %copy.20.live_any, s32[8]{0:T(128)} %owner_any.1, ...), custom_call_target="tpu_custom_call" | custom-call | tf_op jit(solution)/shard_map/pallas_call | solution.py:680
  61.8 2.4 %shard_map.181 = (bf16[256,2048]{1,0:T(8,128)(2,1)}, f32[1,16,2048]{2,1,0:T(8,128)}, f32[1,16,256]{2,1,0:T(8,128)}, f32[1,16,2048]{2,1,0:T(8,128)}, f32[1,16,204...) custom-call(bf16[256,2048]{1,0:T(8,128)(2,1)} %get-tuple-element.14.refs_0_, ...), custom_call_target="tpu_custom_call" | custom-call | tf_op jit(solution)/shard_map/pallas_call | solution.py:751

commit v7 on v5

--- a/solution.py
+++ b/solution.py
@@ -436,8 +436,11 @@
             hand_out(0, half, chunk)
 
     give(0)
+    give(1)
     dv_over(0, odd, 1 - y).wait_recv()
     dv_share(1, odd, 1 - y)
+    for later in range(2, CHUNKS):
+        give(later)
     for dz in range(1, planes):
         source = (f + 2 * dz) % fsdp
         fac_copy(dz, source).wait_recv()
@@ -445,11 +448,8 @@
     dv_near(1 - odd, y).wait_recv()
     send(dv_over(1, 1 - odd, y))
     dv_share(2, 1 - odd, y)
-    give(1)
     dv_over(1, 1 - odd, 1 - y).wait_recv()
     dv_share(3, 1 - odd, 1 - y)
-    for later in range(2, CHUNKS):
-        give(later)
 
     loads["ids"].wait()
     loads["owner"].wait()
@@ -581,22 +581,7 @@
         forward(later)
         multiply(later)
 
-    for dz in range(1, planes):
-        grad_copy(dz, 0, (z + dz) % planes).wait_recv()
-    for name in ("md", "sd", "mu", "su"):
-        loads[name].wait()
-    down_grad = jnp.sum(grecv[:, :, 0:width].astype(jnp.float32), axis=0, keepdims=True)
-    up_grad = jnp.sum(
-        grecv[:, :, width : width + value].astype(jnp.float32), axis=0, keepdims=True
-    )
-    nd_ref[...], nmd_ref[...], nsd_ref[...] = adam_update(
-        fd_ref[...], down_grad, md_ref[...], sd_ref[...]
-    )
-    nu_ref[...], nmu_ref[...], nsu_ref[...] = adam_update(
-        fu_ref[...], up_grad, mu_ref[...], su_ref[...]
-    )
-
-    for chunk in range(CHUNKS):
+    def finish(chunk):
         for half in range(2):
             for core in range(2):
                 stays = jnp.logical_and(odd == c, jnp.logical_and(half == y, core == c))
@@ -614,6 +599,25 @@
                 out_ref[:, start:stop] = (
                     base[half, core, chunk].astype(jnp.float32) + lows[:, start:stop]
                 ).astype(jnp.bfloat16)
+
+    for chunk in range(CHUNKS - 1):
+        finish(chunk)
+    for dz in range(1, planes):
+        grad_copy(dz, 0, (z + dz) % planes).wait_recv()
+    for name in ("md", "sd", "mu", "su"):
+        loads[name].wait()
+    down_grad = jnp.sum(grecv[:, :, 0:width].astype(jnp.float32), axis=0, keepdims=True)
+    up_grad = jnp.sum(
+        grecv[:, :, width : width + value].astype(jnp.float32), axis=0, keepdims=True
+    )
+    nd_ref[...], nmd_ref[...], nsd_ref[...] = adam_update(
+        fd_ref[...], down_grad, md_ref[...], sd_ref[...]
+    )
+    nu_ref[...], nmu_ref[...], nsu_ref[...] = adam_update(
+        fu_ref[...], up_grad, mu_ref[...], su_ref[...]
+    )
+
+    finish(CHUNKS - 1)
 
     for copy, cond in pending:
         if cond is None:

time: 62.6 us -> 63.2 us (level)
  Pallas kernels: 61.1 us -> 61.8 us
    pallas_call x1, Pallas kernels: 58.7 us -> 59.3 us  [fused(): pl.pallas_call(functools.partial(fused_kernel, fsdp, tensor), out_shape=s...]
where the time goes in v7:
time: 63.2 us; the launch traced here: 63 us
  Pallas kernels  61.8 us (98%)
  between operations  1.29 us (2%)
    pallas_call x1, Pallas kernels, fused(): pl.pallas_call(functools.partial(fused_kernel, fsdp, tensor), out_shape=s...  59.3 us
    pallas_call x1, Pallas kernels, fused(): pl.pallas_call(functools.partial(write_kernel, len(shapes)), out_shape=sh...  2.45 us

profile of v7, /device:TPU:21, one launch (start us, length us, event | category | flops | bytes accessed | tf_op | source)
XLA Modules:
  0.0 63.0 jit_solution(11536073636988232014)
XLA Ops:
  1.3 59.3 %shard_map.180 = (bf16[256,2048]{1,0:T(8,128)(2,1)}, f32[1,16,2048]{2,1,0:T(8,128)}, f32[1,16,256]{2,1,0:T(8,128)}, f32[1,16,2048]{2,1,0:T(8,128)}, f32[1,16,204...) custom-call(s32[16]{0:T(128)} %ids_any.1, s32[1]{0:T(128)S(6)} %copy.20.live_any, s32[8]{0:T(128)} %owner_any.1, ...), custom_call_target="tpu_custom_call" | custom-call | tf_op jit(solution)/shard_map/pallas_call | solution.py:678
  60.6 2.4 %shard_map.181 = (bf16[256,2048]{1,0:T(8,128)(2,1)}, f32[1,16,2048]{2,1,0:T(8,128)}, f32[1,16,256]{2,1,0:T(8,128)}, f32[1,16,2048]{2,1,0:T(8,128)}, f32[1,16,204...) custom-call(bf16[256,2048]{1,0:T(8,128)(2,1)} %get-tuple-element.14.refs_0_, ...), custom_call_target="tpu_custom_call" | custom-call | tf_op jit(solution)/shard_map/pallas_call | solution.py:749
